TPU v7x, 32 devices: a whole 2x2x4 slice. The times are simulated.
32 devices in a mesh: gx: 16 (over z, x, core), gz: 2 (over y).
Axes of the slice: x: 2, y: 2, z: 4, core: 2. Of those that a mesh axis runs over, the one named last changes fastest.
Arguments:
- velocity: float32 [2, 2, 1, 4096, 2048], P(None, None, None, 'gx', 'gz'), may hold values from -6 to 6
- previous: float32 [2, 2, 1, 4096, 2048], P(None, None, None, 'gx', 'gz'), may hold values from -12 to 12
- base_flow: float32 [1], replicated, may hold values from -1 to 1
Outputs:
- velocity_next: float32 [2, 2, 1, 4096, 2048], P(None, None, None, 'gx', 'gz')
- nonlinear: float32 [2, 2, 1, 4096, 2048], P(None, None, None, 'gx', 'gz')
All inputs are finite; a program needn't handle non-finite values.
Results may differ from a plain program's by a relative error of at most 0.00014.
Values sent between devices are 32-bit elements; how exact they have to be, the bound alone decides.
A program may use at most 128 MiB of HBM per device.

v0:
```python
import functools
import math

import jax
import jax.numpy as jnp
import numpy as np
from jax import lax
from jax.experimental import pallas as pl
from jax.experimental.pallas import tpu as pltpu
from jax.sharding import PartitionSpec as P

NX = 4096
NZ = 2048


TWO_PI = 2.0 * math.pi
VISCOSITY = 0.05
TIME_STEP = 0.2
GAMMA_NEW = 8.0 / 15.0
ZETA_OLD = -17.0 / 60.0


def partner_2(x, axis, distance):
    return lax.ppermute(x, axis, [(i, i ^ 1 << distance) for i in range(lax.axis_size(axis))])


def exact_einsum(pattern, left_array, right_array):
    return jnp.einsum(
        pattern,
        left_array,
        right_array,
        precision=lax.Precision.HIGHEST,
        preferred_element_type=jnp.float32,
    )


def phase_table(left_ints, right_ints, period, direction):
    phase_angle = (
        direction * TWO_PI / period * (left_ints * right_ints % period).astype(jnp.float32)
    )
    return (jnp.cos(phase_angle), jnp.sin(phase_angle))


def complex_apply(value_real, value_imag, table_real, table_imag, pattern):
    out_real = exact_einsum(pattern, value_real, table_real) - exact_einsum(
        pattern, value_imag, table_imag
    )
    out_imag = exact_einsum(pattern, value_real, table_imag) + exact_einsum(
        pattern, value_imag, table_real
    )
    return (out_real, out_imag)


def residue_of(position, levels):
    reversed_bits = jnp.zeros((), jnp.int32)
    for level in range(levels):
        reversed_bits = reversed_bits + ((position >> level & 1) << levels - 1 - level)
    return reversed_bits


def section_twiddle(position, half_span):
    phase_angle = TWO_PI / (2 * half_span) * (position % half_span).astype(jnp.float32)
    return (jnp.cos(phase_angle), jnp.sin(phase_angle))


def spread_butterfly(values):
    position = lax.axis_index("gx")
    levels = lax.axis_size("gx").bit_length() - 1
    for level in reversed(range(levels)):
        half_span = 1 << level
        partner = partner_2(values, "gx", level)
        upper_half = position >> level & 1 == 1
        cosine, sine_part = section_twiddle(position, half_span)
        difference = partner - values
        rotated = jnp.stack(
            [
                difference[:, 0] * cosine - difference[:, 1] * sine_part,
                difference[:, 0] * sine_part + difference[:, 1] * cosine,
            ],
            axis=1,
        )
        values = jnp.where(upper_half, rotated, values + partner)
    return (values, residue_of(position, levels))


def gather_butterfly(values):
    position = lax.axis_index("gx")
    levels = lax.axis_size("gx").bit_length() - 1
    for level in range(levels):
        half_span = 1 << level
        partner = partner_2(values, "gx", level)
        upper_half = position >> level & 1 == 1
        cosine, sine_part = section_twiddle(position, half_span)
        upper_item = jnp.where(upper_half, values, partner)
        lower_item = jnp.where(upper_half, partner, values)
        turned = jnp.stack(
            [
                upper_item[:, 0] * cosine + upper_item[:, 1] * sine_part,
                upper_item[:, 1] * cosine - upper_item[:, 0] * sine_part,
            ],
            axis=1,
        )
        values = jnp.where(upper_half, lower_item - turned, lower_item + turned)
    return values


def axial_table(residue, mode_count, device_count):
    numbers = jnp.arange(mode_count, dtype=jnp.int32)
    points = residue + device_count * numbers
    cosine, sine_part = phase_table(points[:, None], numbers[None, :], NX, 1.0)
    norm_scale = 1.0 / math.sqrt(NX)
    return (cosine * norm_scale, sine_part * norm_scale)


def span_table(groups, span_size):
    residues = jnp.arange(groups, dtype=jnp.int32)[:, None, None]
    grid_rows = jnp.arange(span_size, dtype=jnp.int32)[None, :, None]
    mode_cols = jnp.arange(span_size, dtype=jnp.int32)[None, None, :]
    cosine, sine_part = phase_table(mode_cols, residues + groups * grid_rows, NZ, 1.0)
    norm_scale = 1.0 / math.sqrt(NZ)
    return (cosine * norm_scale, sine_part * norm_scale)


def spanwise_work(received):
    fields, pair_size, planes, row_count, extent = received.shape
    groups = lax.axis_size("gz")
    span_size = extent // groups
    blocks = received.reshape(fields, pair_size, planes, row_count, groups, span_size)
    group_ids = jnp.arange(groups, dtype=jnp.int32)
    mix_real, mix_imag = phase_table(group_ids[:, None], group_ids[None, :], groups, 1.0)
    section_real, section_imag = complex_apply(
        blocks[:, 0], blocks[:, 1], mix_real, mix_imag, "fylcj,rc->fylrj"
    )
    table_real, table_imag = span_table(groups, span_size)
    physical = exact_einsum("fylrj,rtj->fylrt", section_real, table_real) - exact_einsum(
        "fylrj,rtj->fylrt", section_imag, table_imag
    )
    products = jnp.stack(
        [physical[0] * physical[0], physical[0] * physical[1], physical[1] * physical[1]]
    )
    back_real = exact_einsum("pylrt,rtj->pylrj", products, table_real)
    back_imag = -exact_einsum("pylrt,rtj->pylrj", products, table_imag)
    out_real, out_imag = complex_apply(back_real, back_imag, mix_real, -mix_imag, "pylrj,cr->pylcj")
    spectra = jnp.stack([out_real, out_imag], axis=1)
    return spectra.reshape(3, pair_size, planes, row_count, extent)


def span_round(values, work):
    span_spectra = work(lax.all_to_all(values, "gz", split_axis=3, concat_axis=4, tiled=True))
    return lax.all_to_all(span_spectra, "gz", split_axis=4, concat_axis=3, tiled=True)


def signed_block(start, mode_count, extent):
    numbers = start + jnp.arange(mode_count, dtype=jnp.int32)
    return jnp.where(2 * numbers < extent, numbers, numbers - extent)


def local(velocity, previous, base_flow):
    mode_count = velocity.shape[3]
    span_size = velocity.shape[4]
    device_count = lax.axis_size("gx")
    spread, residue = spread_butterfly(velocity)
    table_real, table_imag = axial_table(residue, mode_count, device_count)
    along_real, along_imag = complex_apply(
        spread[:, 0], spread[:, 1], table_real, table_imag, "fymq,sm->fysq"
    )
    physical_along = jnp.stack([along_real, along_imag], axis=1)
    returned = span_round(physical_along, spanwise_work)
    local_real, local_imag = complex_apply(
        returned[:, 0], returned[:, 1], table_real.T, -table_imag.T, "fysq,ms->fymq"
    )
    local_spectra = jnp.stack([local_real, local_imag], axis=1)
    product_spectra = gather_butterfly(local_spectra)
    modes_along = signed_block(lax.axis_index("gx") * mode_count, mode_count, NX)
    modes_across = signed_block(lax.axis_index("gz") * span_size, span_size, NZ)
    wave_along = (modes_along.astype(jnp.float32) * (TWO_PI / NX))[:, None]
    wave_across = (modes_across.astype(jnp.float32) * (TWO_PI / NZ))[None, :]
    keep = jnp.logical_and(
        (3 * jnp.abs(modes_along) < NX)[:, None], (3 * jnp.abs(modes_across) < NZ)[None, :]
    ).astype(jnp.float32)
    shear = base_flow[:, None, None] * wave_along[None]
    prod_real = product_spectra[:, 0]
    prod_imag = product_spectra[:, 1]
    first_real = (
        keep * (wave_along * prod_imag[0] + wave_across * prod_imag[1]) + shear * velocity[0, 1]
    )
    first_imag = (
        -keep * (wave_along * prod_real[0] + wave_across * prod_real[1]) - shear * velocity[0, 0]
    )
    second_real = (
        keep * (wave_along * prod_imag[1] + wave_across * prod_imag[2]) + shear * velocity[1, 1]
    )
    second_imag = (
        -keep * (wave_along * prod_real[1] + wave_across * prod_real[2]) - shear * velocity[1, 0]
    )
    nonlinear = jnp.stack(
        [jnp.stack([first_real, first_imag]), jnp.stack([second_real, second_imag])]
    )
    damping = jnp.exp(-VISCOSITY * (wave_along * wave_along + wave_across * wave_across))
    advanced = damping * (velocity + TIME_STEP * (GAMMA_NEW * nonlinear + ZETA_OLD * previous))
    return (advanced, nonlinear)


XR = 16
XS = NX // XR
ZR = 8
ZS = NZ // ZR
LOW = (0, 1, 2)
HIGH = (5, 6, 7)
MIB = 1 << 20
PIECES = 2


def split_table(table):
    high = table.astype(np.float32).astype(jnp.bfloat16)
    low = (table - high.astype(np.float64)).astype(np.float32).astype(jnp.bfloat16)
    return high, low


def z_table():
    r = np.arange(ZR)[:, None, None]
    b = np.arange(ZS)[None, :, None]
    s = np.arange(ZS)[None, None, :]
    angle = TWO_PI / NZ * ((b * (r + ZR * s)) % NZ)
    cos, sin = np.cos(angle) / math.sqrt(NZ), np.sin(angle) / math.sqrt(NZ)
    return split_table(np.concatenate([cos, sin], axis=2))


def x_table():
    r = np.arange(XR)[:, None, None]
    s = np.arange(XS)[None, :, None]
    m = np.arange(XS)[None, None, :]
    angle = TWO_PI / NX * ((m * (r + XR * s)) % NX)
    cos, sin = np.cos(angle) / math.sqrt(NX), np.sin(angle) / math.sqrt(NX)
    return split_table(np.concatenate([cos, -sin], axis=2))


def turn(value, numerator, size, sign):
    re, im = value
    numerator = numerator % size
    if numerator == 0:
        return re, im
    if 4 * numerator == size:
        return (-im, re) if sign > 0 else (im, -re)
    if 8 * numerator == size:
        h = math.sqrt(0.5)
        return ((re - im) * h, (re + im) * h) if sign > 0 else ((re + im) * h, (im - re) * h)
    if 8 * numerator == 3 * size:
        h = math.sqrt(0.5)
        return ((-re - im) * h, (re - im) * h) if sign > 0 else ((im - re) * h, (-re - im) * h)
    c = math.cos(TWO_PI * numerator / size)
    s = sign * math.sin(TWO_PI * numerator / size)
    return re * c - im * s, re * s + im * c


def small_dft(values, sign):
    size = len(values)
    if size == 1:
        return values
    even = small_dft(values[0::2], sign)
    odd = small_dft(values[1::2], sign)
    half = size // 2
    out = [None] * size
    for i in range(half):
        re, im = turn(odd[i], i, size, sign)
        out[i] = (even[i][0] + re, even[i][1] + im)
        out[i + half] = (even[i][0] - re, even[i][1] - im)
    return out


def parts_of(value):
    high = value.astype(jnp.bfloat16)
    return high, (value - high.astype(jnp.float32)).astype(jnp.bfloat16)


def dot3(a_high, a_low, b_high, b_low, dims):
    def dot(a, b):
        return lax.dot_general(a, b, (dims, ((), ())), preferred_element_type=jnp.float32)

    return dot(a_high, b_high) + (dot(a_high, b_low) + dot(a_low, b_high))


def merge(first, second, low_half):
    return (
        jnp.where(low_half, first, pltpu.roll(second, 64, 1)),
        jnp.where(low_half, pltpu.roll(first, 64, 1), second),
    )


def z_inverse_kernel(half_ref, own_ref, other_ref, high_ref, low_ref, out_ref, th_ref, tl_ref):
    rows = own_ref.shape[2]
    step = 16
    first = half_ref[0] == 0
    for c in range(2):
        def body(i, carry):
            at = pl.multiple_of(i * step, step)
            for lane in range(0, ZS, 128):
                values = [None] * ZR
                for a in range(ZR // 2):
                    to = (pl.ds(at, step), pl.ds(a * ZS + lane, 128))
                    own = [own_ref[(c, p) + to] for p in range(2)]
                    other = [other_ref[(c, p) + to] for p in range(2)]
                    values[a] = tuple(jnp.where(first, x, y) for x, y in zip(own, other))
                    values[a + ZR // 2] = tuple(jnp.where(first, y, x) for x, y in zip(own, other))
                for r, pair in enumerate(small_dft(values, 1)):
                    for p in range(2):
                        high, low = parts_of(pair[p])
                        line = pl.ds((2 * p + c) * rows + at, step)
                        th_ref[r, line, pl.ds(lane, 128)] = high
                        tl_ref[r, line, pl.ds(lane, 128)] = low
            return carry
        lax.fori_loop(0, rows // step, body, 0)

    def group(r, carry):
        both = dot3(th_ref[r], tl_ref[r], high_ref[r], low_ref[r], ((1,), (0,)))
        real, imag = both[: 2 * rows], both[2 * rows :]
        done = jnp.concatenate(
            [real[:, :ZS] - imag[:, ZS:], real[:, ZS:] + imag[:, :ZS]], axis=1
        )
        low_half = lax.broadcasted_iota(jnp.int32, (rows, 128), 1) < 64
        for p in range(2):
            for t in range(2):
                at = p * ZS + t * 128
                even, odd = merge(done[:rows, at : at + 128], done[rows:, at : at + 128], low_half)
                out_ref[r, 2 * t, p] = even
                out_ref[r, 2 * t + 1, p] = odd
        return carry
    lax.fori_loop(0, ZR, group, 0)


def x_kernel(*refs):
    v_refs, (ih_ref, il_ref, fh_ref, fl_ref) = refs[:PIECES], refs[PIECES : PIECES + 4]
    out_refs = refs[PIECES + 4 : 2 * PIECES + 4]
    th_ref, tl_ref, u_ref = refs[2 * PIECES + 4 :]
    rows = v_refs[0].shape[3]
    step = 16
    for r, h in ((r, h) for r in range(2) for h in range(PIECES)):
        v_ref, base = v_refs[h], (r * PIECES + h) * rows

        def body(i, carry):
            at = pl.multiple_of(i * step, step)
            values = [
                tuple(v_ref[g, r, p, pl.ds(at, step), :] for p in range(2)) for g in range(XR)
            ]
            for res, pair in enumerate(small_dft(values, 1)):
                for p in range(2):
                    high, low = parts_of(pair[p])
                    th_ref[res, pl.ds(p * XS + base + at, step), :] = high
                    tl_ref[res, pl.ds(p * XS + base + at, step), :] = low
            return carry
        lax.fori_loop(0, rows // step, body, 0)

    def residue(res, carry):
        field = dot3(ih_ref[res], il_ref[res], th_ref[res], tl_ref[res], ((1,), (0,)))
        swapped = pltpu.roll(field, 64, 1)
        products = jnp.concatenate([field * field, field * swapped], axis=1)
        high, low = parts_of(products)
        u_ref[res] = dot3(fh_ref[res], fl_ref[res], high, low, ((1,), (0,)))
        return carry
    lax.fori_loop(0, XR, residue, 0)

    low_half = lax.broadcasted_iota(jnp.int32, (8, 128), 1) < 64
    for r, n in ((r, n) for r in range(2) for n in range(PIECES)):
        out_ref, base = out_refs[n], (r * PIECES + n) * rows

        def back(i, carry):
            at = pl.multiple_of(i * 8, 8)
            for h in range(2):
                values = [
                    tuple(
                        u_ref[res, pl.ds(p * XS + base + at, 8), pl.ds(h * 128, 128)]
                        for p in range(2)
                    )
                    for res in range(XR)
                ]
                for g, (re, im) in enumerate(small_dft(values, -1)):
                    if h == 0:
                        out_ref[g, r, 0, pl.ds(at, 8), :] = re
                        out_ref[g, r, 1, pl.ds(at, 8), :] = im
                    else:
                        out_ref[g, r, 2, pl.ds(at, 8), :] = jnp.where(low_half, re, im)
            return carry
        lax.fori_loop(0, rows // 8, back, 0)


def z_forward_kernel(half_ref, v_ref, high_ref, low_ref, wave_ref, keep_ref, own_ref, other_ref, w_ref):
    lower = half_ref[0] == 0
    rows = v_ref.shape[3]
    low_half = lax.broadcasted_iota(jnp.int32, (rows, 128), 1) < 64

    def group(r, carry):
        real, imag, mixed = ([v_ref[r, j, x] for j in range(4)] for x in range(3))
        p0r, p2r, p0i, p2i, p1r, p1i = [], [], [], [], [], []
        for source, first, second in ((real, p0r, p2r), (imag, p0i, p2i), (mixed, p1r, p1i)):
            for t in range(2):
                a, b = merge(source[2 * t], source[2 * t + 1], low_half)
                first.append(a)
                second.append(b)
        lines = jnp.concatenate(
            [jnp.concatenate(x, axis=1) for x in (p0r, p1r, p2r, p0i, p1i, p2i)], axis=0
        )
        high, low = parts_of(lines)
        cos, sin = (
            dot3(high, low, high_ref[r, :, at : at + ZS], low_ref[r, :, at : at + ZS], ((1,), (1,)))
            for at in (0, ZS)
        )
        w_ref[r, :, :ZS] = cos[: 3 * rows] + sin[3 * rows :]
        w_ref[r, :, ZS:] = cos[3 * rows :] - sin[: 3 * rows]
        return carry
    lax.fori_loop(0, ZR, group, 0)

    def body(i, carry):
        at = pl.multiple_of(i * 8, 8)
        wave_along = wave_ref[pl.ds(at, 8), :]
        keep_along = keep_ref[pl.ds(at, 8), :]
        for lane in range(0, ZS, 128):
            spectra = []
            for j in range(3):
                values = [
                    tuple(
                        w_ref[r, pl.ds(j * rows + at, 8), pl.ds(p * ZS + lane, 128)]
                        for p in range(2)
                    )
                    for r in range(ZR)
                ]
                spectra.append(small_dft(values, -1))
            for place in range(len(LOW)):
                terms = []
                for half, groups in enumerate((LOW, HIGH)):
                    a = groups[place]
                    start = a * ZS + lane - (NZ if half else 0)
                    mode = start + lax.broadcasted_iota(jnp.int32, (8, 128), 1)
                    wave_across = mode.astype(jnp.float32) * (TWO_PI / NZ)
                    keep = jnp.logical_and(3 * jnp.abs(mode) < NZ, keep_along > 0.5)
                    (ar, ai), (br, bi), (cr, ci) = (x[a] for x in spectra)
                    terms.append(
                        [
                            jnp.where(keep, wave_along * ai + wave_across * bi, 0.0),
                            jnp.where(keep, -(wave_along * ar + wave_across * br), 0.0),
                            jnp.where(keep, wave_along * bi + wave_across * ci, 0.0),
                            jnp.where(keep, -(wave_along * br + wave_across * cr), 0.0),
                        ]
                    )
                to = (pl.ds(at, 8), pl.ds(place * ZS + lane, 128))
                for x in range(4):
                    own_ref[(x,) + to] = jnp.where(lower, terms[0][x], terms[1][x])
                    other_ref[(x,) + to] = jnp.where(lower, terms[1][x], terms[0][x])
        return carry
    lax.fori_loop(0, rows // 8, body, 0)


def advance_kernel(half_ref, base_ref, v_ref, old_ref, *refs):
    own_refs, got_refs = refs[:PIECES], refs[PIECES : 2 * PIECES]
    along_ref, across_ref, next_ref, non_ref = refs[2 * PIECES :]
    place = pl.program_id(0)
    is_own = place // PIECES == half_ref[0]
    piece = lax.rem(place, PIECES)
    rows, extent = v_ref.shape[2:]
    wave_along = along_ref[:, :1]
    wave_across = across_ref[:1, :]
    damping = jnp.exp(-VISCOSITY * (wave_along * wave_along + wave_across * wave_across))
    shear = base_ref[0] * wave_along
    empty = jnp.zeros((rows, extent - own_refs[0].shape[2]), jnp.float32)
    for c in range(2):
        for p in range(2):
            term = None
            for h in range(PIECES):
                this = jnp.where(is_own, own_refs[h][2 * c + p], got_refs[h][2 * c + p])
                term = this if term is None else jnp.where(piece == h, this, term)
            term = jnp.where(
                half_ref[0] == 0,
                jnp.concatenate([term, empty], axis=1),
                jnp.concatenate([empty, term], axis=1),
            )
            other = shear * v_ref[c, 1 - p]
            result = term + other if p == 0 else term - other
            non_ref[c, p] = result
            next_ref[c, p] = damping * (
                v_ref[c, p] + TIME_STEP * (GAMMA_NEW * result + ZETA_OLD * old_ref[c, p])
            )


def whole(*_):
    return pl.BlockSpec(memory_space=pltpu.VMEM)


def params(limit):
    return pltpu.CompilerParams(vmem_limit_bytes=limit * MIB)


def kept(block, block_rows):
    start = block * block_rows
    return jnp.logical_or(3 * start < NX, 3 * (NX - start - block_rows + 1) < NX)


def exchange_kernel(block_rows, src_ref, dst_ref, send_sems, recv_sems, own_sem):
    across = lax.axis_size("gz")
    count = lax.axis_size("gx") * across
    me = lax.axis_index("gx") * across + lax.axis_index("gz")

    def device(t):
        return (t // across, lax.rem(t, across))

    def wanted(t):
        return kept(t, block_rows) if block_rows else t >= 0

    barrier = pltpu.get_barrier_semaphore()

    def greet(i, carry):
        pl.semaphore_signal(
            barrier,
            inc=1,
            device_id=device(lax.rem(me + i, count)),
            device_id_type=pl.DeviceIdType.MESH,
        )
        return carry

    lax.fori_loop(1, count, greet, 0)
    pl.semaphore_wait(barrier, count - 1)

    def copy(i):
        t = lax.rem(me + i, count)
        return pltpu.make_async_remote_copy(
            src_ref=src_ref.at[t],
            dst_ref=dst_ref.at[me],
            send_sem=send_sems.at[i],
            recv_sem=recv_sems.at[i],
            device_id=device(t),
            device_id_type=pl.DeviceIdType.MESH,
        )

    def start(i, carry):
        @pl.when(wanted(lax.rem(me + i, count)))
        def _():
            copy(i).start()

        return carry

    lax.fori_loop(1, count, start, 0)
    own = pltpu.make_async_copy(src_ref.at[me], dst_ref.at[me], own_sem)
    own.start()
    own.wait()

    def finish(i, carry):
        @pl.when(wanted(lax.rem(me + i, count)))
        def _():
            copy(i).wait_send()

        @pl.when(wanted(me))
        def _():
            copy(i).wait_recv()

        return carry

    lax.fori_loop(1, count, finish, 0)


def exchange(value, number, block_rows=0):
    count = value.shape[0]
    return pl.pallas_call(
        functools.partial(exchange_kernel, block_rows),
        out_shape=jax.ShapeDtypeStruct(value.shape, value.dtype),
        in_specs=[pl.BlockSpec(memory_space=pl.ANY)],
        out_specs=pl.BlockSpec(memory_space=pl.ANY),
        scratch_shapes=[
            pltpu.SemaphoreType.DMA((count,)),
            pltpu.SemaphoreType.DMA((count,)),
            pltpu.SemaphoreType.DMA,
        ],
        compiler_params=pltpu.CompilerParams(collective_id=number, has_side_effects=True),
        cost_estimate=pl.CostEstimate(flops=0, bytes_accessed=64 * value.size, transcendentals=0),
        name="exchange_" + str(number),
    )(value)


def lines_local(velocity, previous, base_flow):
    velocity, previous = velocity[:, :, 0], previous[:, :, 0]
    mode_count, extent = velocity.shape[2:]
    rows = mode_count // 2
    gx, gz = lax.axis_index("gx"), lax.axis_index("gz")
    f32, bf16 = jnp.float32, jnp.bfloat16
    zh, zl = z_table()
    xh, xl = x_table()
    fh, fl = np.swapaxes(xh, 1, 2), np.swapaxes(xl, 1, 2)

    piece = rows // PIECES
    half = gz.astype(jnp.int32)[None]
    scalar = pl.BlockSpec(memory_space=pltpu.SMEM)
    swap = [(0, 1), (1, 0)]
    got, swapped = [], []
    for h in range(PIECES):
        part = lax.dynamic_slice_in_dim(velocity, (1 - gz) * rows + h * piece, piece, axis=2)
        if h:
            part, got[h - 1] = lax.optimization_barrier((part, got[h - 1]))
        got.append(lax.ppermute(part, "gz", swap))
    for h in range(PIECES):
        mine = lax.dynamic_slice_in_dim(velocity, gz * rows + h * piece, piece, axis=2)
        if h:
            mine, swapped[h - 1] = lax.optimization_barrier((mine, swapped[h - 1]))
        along_z = pl.pallas_call(
            z_inverse_kernel,
            out_shape=jax.ShapeDtypeStruct((ZR, 4, 2, piece, 128), f32),
            in_specs=[scalar] + [whole()] * 4,
            out_specs=whole(),
            scratch_shapes=[pltpu.VMEM((ZR, 4 * piece, ZS), bf16)] * 2,
            compiler_params=params(40),
            name="z_inverse",
        )(half, mine, got[h], zh, zl)
        swapped.append(exchange(along_z.reshape(32, 2, piece, 128), 1 + h))
    worked = pl.pallas_call(
        x_kernel,
        out_shape=[jax.ShapeDtypeStruct((XR, 2, 3, piece, 128), f32)] * PIECES,
        in_specs=[whole()] * (PIECES + 4),
        out_specs=[whole()] * PIECES,
        scratch_shapes=[pltpu.VMEM((XR, 2 * XS, 128), bf16)] * 2
        + [pltpu.VMEM((XR, 2 * XS, 256), f32)],
        compiler_params=params(56),
        name="x_work",
    )(*(x.reshape(XR, 2, 2, piece, 128) for x in swapped), xh, xl, fh, fl)

    def modes(start, count, size):
        numbers = start + jnp.arange(count, dtype=jnp.int32)
        return jnp.where(2 * numbers < size, numbers, numbers - size)

    own = modes(gx * mode_count + gz * rows, rows, NX)[:, None]
    own_wave = jnp.broadcast_to(own.astype(f32) * (TWO_PI / NX), (rows, 128))
    own_keep = jnp.broadcast_to((3 * jnp.abs(own) < NX).astype(f32), (rows, 128))
    active = len(LOW) * ZS
    own_terms, got_terms = [], []
    for h in range(PIECES):
        sent = worked[h].reshape(32, 3, piece, 128)
        if h:
            sent, own_terms[h - 1] = lax.optimization_barrier((sent, own_terms[h - 1]))
        returned = exchange(sent, 1 + PIECES + h, rows)
        at = slice(h * piece, (h + 1) * piece)
        mine, other = pl.pallas_call(
            z_forward_kernel,
            out_shape=[jax.ShapeDtypeStruct((4, piece, active), f32)] * 2,
            in_specs=[scalar] + [whole()] * 5,
            out_specs=[whole()] * 2,
            scratch_shapes=[pltpu.VMEM((ZR, 3 * piece, 2 * ZS), f32)],
            compiler_params=params(40),
            name="z_forward",
        )(half, returned.reshape(ZR, 4, 3, piece, 128), zh, zl, own_wave[at], own_keep[at])
        own_terms.append(mine)
        got_terms.append(lax.ppermute(other, "gz", swap))

    along = modes(gx * mode_count, mode_count, NX).astype(f32) * (TWO_PI / NX)
    across = modes(gz * extent, extent, NZ).astype(f32) * (TWO_PI / NZ)
    block = piece
    field = pl.BlockSpec((2, 2, block, extent), lambda i: (0, 0, i, 0))
    advanced, nonlinear = pl.pallas_call(
        advance_kernel,
        grid=(mode_count // block,),
        out_shape=[jax.ShapeDtypeStruct(velocity.shape, f32)] * 2,
        in_specs=[
            scalar,
            scalar,
            field,
            field,
            *([pl.BlockSpec((4, block, active), lambda i: (0, 0, 0))] * (2 * PIECES)),
            pl.BlockSpec((block, 128), lambda i: (i, 0)),
            pl.BlockSpec((8, extent), lambda i: (0, 0)),
        ],
        out_specs=[field, field],
        compiler_params=params(48),
        name="advance",
    )(
        half,
        base_flow,
        velocity,
        previous,
        *own_terms,
        *got_terms,
        jnp.broadcast_to(along[:, None], (mode_count, 128)),
        jnp.broadcast_to(across[None], (8, extent)),
    )
    return advanced[:, :, None], nonlinear[:, :, None]


def solution(mesh):
    in_specs = (P(None, None, None, "gx", "gz"), P(None, None, None, "gx", "gz"), P())
    out_specs = (P(None, None, None, "gx", "gz"), P(None, None, None, "gx", "gz"))
    fits = mesh.shape["gx"] == XR and mesh.shape["gz"] == 2
    work = lines_local if fits else local
    return jax.shard_map(work, mesh=mesh, in_specs=in_specs, out_specs=out_specs, check_vma=False)
```

profile of v0, /device:TPU:12, one launch (start us, length us, event | category | flops | bytes accessed | tf_op | source)
XLA Modules:
  0.0 350.2 jit_solution(10722207325772673768)
XLA Ops:
  0.7 4.1 %dynamic-slice_bitcast_fusion = (f32[2,2,64,1024]{3,2,1,0:T(8,128)S(1)}, f32[2,2,64,1024]{3,2,1,0:T(8,128)}, f32[2,2,64,1024]{3,2,1,0:T(8,128)S(1)}, f32[2,2,64,1024]{3,2,1,0:T(8,128)}) fusion(f32[2,2,1,256,1024]{4,3,2,1,0:T(8,128)} %param.9, s32[]{:T(128)S(6)} %select_n.46, s32[]{:T(128)S(6)} %select_n.44, s32[]{:T(128)S(6)} %select_n.43, s32[]{:T(128)S(6)} %select_n.45), kind=kLoop, calls=%fused_computation | loop fusion | bytes 8388624 | tf_op jit(solution)/shard_map/dynamic_slice | solution.py:592
  4.8 0.5 collective-permute-start
  5.3 24.4 %collective-permute-done.other_ref = f32[2,2,64,1024]{3,2,1,0:T(8,128)S(1)} collective-permute-done((f32[2,2,64,1024]{3,2,1,0:T(8,128)S(1)}, f32[2,2,64,1024]{3,2,1,0:T(8,128)S(1)}, u32[]{:S(2)}, u32[]{:S(2)}) %collective-permute-start) | collective-permute-done | bytes 1048608 | tf_op jit(solution)/shard_map/ppermute | solution.py:595
  29.7 1.0 copy-done.10
  30.6 0.5 collective-permute-start.1
  31.2 0.1 slice_bitcast_fusion.1
  31.2 0.1 slice_bitcast_fusion
  31.3 1.6 copy-done.1
  32.9 1.2 copy-done.9
  34.1 1.2 copy-done.11
  35.4 4.5 %z_inverse.2 = f32[8,4,2,64,128]{4,3,2,1,0:T(8,128)S(1)} custom-call(s32[1]{0:T(128)} %bitcast.half_ref, f32[2,2,64,1024]{3,2,1,0:T(8,128)S(1)} %copy-done.9, f32[2,2,64,1024]{3,2,1,0:T(8,128)S(1)} %copy-done.11, bf16[8,256,512]{2,1,0:T(8,128)(2,1)S(1)} %copy-done.1, bf16[8,256,512]{2,1,0:T(8,128)(2,1)S(1)} %copy-done), custom_call_target="tpu_custom_call" | custom-call | tf_op jit(solution)/shard_map/z_inverse/pallas_call | solution.py:600
  39.9 1.3 copy-done.7
  41.2 51.1 %exchange_1.1 = f32[32,2,64,128]{3,2,1,0:T(8,128)} custom-call(f32[32,2,64,128]{3,2,1,0:T(8,128)} %bitcast.35), custom_call_target="tpu_custom_call" | custom-call | bytes 33554432 | tf_op jit(solution)/shard_map/exchange_1/pallas_call | solution.py:560
  92.4 1.6 copy-done.2
  94.0 5.7 %z_inverse.3 = f32[8,4,2,64,128]{4,3,2,1,0:T(8,128)S(1)} custom-call(s32[1]{0:T(128)} %bitcast.half_ref, f32[2,2,64,1024]{3,2,1,0:T(8,128)S(1)} %get-tuple-element.18.own_ref, f32[2,2,64,1024]{3,2,1,0:T(8,128)} %collective-permute-done.1.other_ref, bf16[8,256,512]{2,1,0:T(8,128)(2,1)S(1)} %copy-done.2, bf16[8,256,512]{2,1,0:T(8,128)(2,1)S(1)} %copy-done), custom_call_target="tpu_custom_call" | custom-call | tf_op jit(solution)/shard_map/z_inverse/pallas_call | solution.py:600
  99.7 1.3 copy-done.8
  101.1 50.6 %exchange_2.1 = f32[32,2,64,128]{3,2,1,0:T(8,128)} custom-call(f32[32,2,64,128]{3,2,1,0:T(8,128)} %bitcast.36), custom_call_target="tpu_custom_call" | custom-call | bytes 33554432 | tf_op jit(solution)/shard_map/exchange_2/pallas_call | solution.py:560
  151.6 27.9 %x_work.1 = (f32[16,2,3,64,128]{4,3,2,1,0:T(8,128)}, f32[16,2,3,64,128]{4,3,2,1,0:T(8,128)}) custom-call(f32[16,2,2,64,128]{4,3,2,1,0:T(8,128)} %bitcast.38, f32[16,2,2,64,128]{4,3,2,1,0:T(8,128)} %bitcast.39, bf16[16,256,512]{2,1,0:T(8,128)(2,1)} %constant.63.clone.refs_2_, bf16[16,256,512]{2,1,0:T(8,128)(2,1)} %constant.64.clone.refs_3_, ...), custom_call_target="tpu_custom_call" | custom-call | tf_op jit(solution)/shard_map/x_work/pallas_call | solution.py:610
  179.6 61.5 %exchange_3.1 = f32[32,3,64,128]{3,2,1,0:T(8,128)} custom-call(f32[32,3,64,128]{3,2,1,0:T(8,128)} %bitcast.42), custom_call_target="tpu_custom_call" | custom-call | bytes 50331648 | tf_op jit(solution)/shard_map/exchange_3/pallas_call | solution.py:560
  241.1 0.1 broadcast_in_dim.38.keep_ref
  241.3 1.6 copy-done.3
  242.9 1.9 copy-done.6
  244.8 5.9 %z_forward.2 = (f32[4,64,768]{2,1,0:T(8,128)S(1)}, f32[4,64,768]{2,1,0:T(8,128)}) custom-call(s32[1]{0:T(128)} %bitcast.half_ref, f32[8,4,3,64,128]{4,3,2,1,0:T(8,128)S(1)} %bitcast.34, bf16[8,256,512]{2,1,0:T(8,128)(2,1)S(1)} %copy-done.3, bf16[8,256,512]{2,1,0:T(8,128)(2,1)S(1)} %copy-done, f32[64,128]{1,0:T(8,128)S(1)} %broadcast_in_dim.37.wave_ref, ...), custom_call_target="tpu_custom_call" | custom-call | tf_op jit(solution)/shard_map/z_forward/pallas_call | solution.py:636
  250.6 60.1 %exchange_4.1 = f32[32,3,64,128]{3,2,1,0:T(8,128)} custom-call(f32[32,3,64,128]{3,2,1,0:T(8,128)} %bitcast.41), custom_call_target="tpu_custom_call" | custom-call | bytes 50331648 | tf_op jit(solution)/shard_map/exchange_4/pallas_call | solution.py:560
  310.8 1.6 copy-done.4
  312.4 1.9 copy-done.5
  314.3 5.9 %z_forward.3 = (f32[4,64,768]{2,1,0:T(8,128)S(1)}, f32[4,64,768]{2,1,0:T(8,128)}) custom-call(s32[1]{0:T(128)} %bitcast.half_ref, f32[8,4,3,64,128]{4,3,2,1,0:T(8,128)S(1)} %bitcast.33, bf16[8,256,512]{2,1,0:T(8,128)(2,1)S(1)} %copy-done.4, bf16[8,256,512]{2,1,0:T(8,128)(2,1)S(1)} %copy-done, f32[64,128]{1,0:T(8,128)S(1)} %broadcast_in_dim.39.wave_ref, ...), custom_call_target="tpu_custom_call" | custom-call | tf_op jit(solution)/shard_map/z_forward/pallas_call | solution.py:636
  320.2 0.9 copy-done.12
  321.7 18.6 %collective-permute-done.3.refs_3_ = f32[4,64,768]{2,1,0:T(8,128)S(1)} collective-permute-done((f32[4,64,768]{2,1,0:T(8,128)}, f32[4,64,768]{2,1,0:T(8,128)S(1)}, u32[]{:S(2)}, u32[]{:S(2)}) %collective-permute-start.3) | collective-permute-done | bytes 786464 | tf_op jit(solution)/shard_map/ppermute | solution.py:646
  340.4 0.1 broadcast_in_dim.41.refs_4_
  340.5 1.1 copy-done.13
  341.6 8.6 %advance.1 = (f32[2,2,256,1024]{3,2,1,0:T(8,128)}, f32[2,2,256,1024]{3,2,1,0:T(8,128)}) custom-call(s32[1]{0:T(128)} %bitcast.half_ref, f32[1]{0:T(128)S(6)} %copy.13.base_ref, f32[2,2,256,1024]{3,2,1,0:T(8,128)} %bitcast.37, f32[2,2,256,1024]{3,2,1,0:T(8,128)} %bitcast.40, f32[4,64,768]{2,1,0:T(8,128)S(1)} %get-tuple-element.23.refs_0_, ...), custom_call_target="tpu_custom_call" | custom-call | tf_op jit(solution)/shard_map/advance/pallas_call | solution.py:652
  (27 shorter events, 0.3 us)
Async XLA Ops:
  0.6 30.7 %copy-start = (bf16[8,256,512]{2,1,0:T(8,128)(2,1)S(1)}, bf16[8,256,512]{2,1,0:T(8,128)(2,1)}, u32[]{:S(2)}) copy-start(bf16[8,256,512]{2,1,0:T(8,128)(2,1)} %constant.62.clone.low_ref) | copy-start | bytes 6291460
  4.8 24.9 %collective-permute-start = (f32[2,2,64,1024]{3,2,1,0:T(8,128)S(1)}, f32[2,2,64,1024]{3,2,1,0:T(8,128)S(1)}, u32[]{:S(2)}, u32[]{:S(2)}) collective-permute-start(f32[2,2,64,1024]{3,2,1,0:T(8,128)S(1)} %get-tuple-element.32), channel_id=1, source_target_pairs={{0,1},{1,0},{2,3},{3,2},{4,5},{5,4},{6,7},{7,6},{8,9},{9,8},{10,11... | collective-permute-start | bytes 3145736 | tf_op jit(solution)/shard_map/ppermute | solution.py:595
  29.7 1.0 copy-start.10
  30.6 61.7 %collective-permute-start.1 = (f32[2,2,64,1024]{3,2,1,0:T(8,128)}, f32[2,2,64,1024]{3,2,1,0:T(8,128)}, u32[]{:S(2)}, u32[]{:S(2)}) collective-permute-start(f32[2,2,64,1024]{3,2,1,0:T(8,128)} %get-tuple-element.19), channel_id=1, source_target_pairs={{0,1},{1,0},{2,3},{3,2},{4,5},{5,4},{6,7},{7,6},{8,9},{9,8},{10,11... | collective-permute-start | bytes 3145736 | tf_op jit(solution)/shard_map/ppermute | solution.py:595
  31.3 1.6 copy-start.1
  32.9 1.2 copy-start.9
  34.1 1.2 copy-start.11
  39.9 1.3 copy-start.7
  92.4 1.6 copy-start.2
  99.7 1.3 copy-start.8
  241.3 1.6 copy-start.3
  242.9 1.9 copy-start.6
  250.6 71.1 %collective-permute-start.2 = (f32[4,64,768]{2,1,0:T(8,128)}, f32[4,64,768]{2,1,0:T(8,128)}, u32[]{:S(2)}, u32[]{:S(2)}) collective-permute-start(f32[4,64,768]{2,1,0:T(8,128)} %get-tuple-element.26), channel_id=1, source_target_pairs={{0,1},{1,0},{2,3},{3,2},{4,5},{5,4},{6,7},{7,6},{8,9},{9,8},{10,11... | collective-permute-start | bytes 2359304 | tf_op jit(solution)/shard_map/ppermute | solution.py:646
  310.8 1.6 copy-start.4
  312.4 1.9 copy-start.5
  320.2 0.9 copy-start.12
  321.0 19.3 %collective-permute-start.3 = (f32[4,64,768]{2,1,0:T(8,128)}, f32[4,64,768]{2,1,0:T(8,128)S(1)}, u32[]{:S(2)}, u32[]{:S(2)}) collective-permute-start(f32[4,64,768]{2,1,0:T(8,128)} %get-tuple-element.27), channel_id=1, source_target_pairs={{0,1},{1,0},{2,3},{3,2},{4,5},{5,4},{6,7},{7,6},{8,9},{9,8},{10,11... | collective-permute-start | bytes 2359304 | tf_op jit(solution)/shard_map/ppermute | solution.py:646
  340.4 1.1 copy-start.13
where the time goes:
time: 351 us; the launch traced here: 350 us
  Pallas kernels  282 us (80%)
  waiting for transfers between devices  43 us (12%)
  local copies, waits for them, and re-layouts  22.9 us (7%)
    pallas_call x4, Pallas kernels, exchange(): pl.pallas_call(functools.partial(exchange_kernel, block_rows), out_shape=...  223 us
    pallas_call x1, Pallas kernels, lines_local(): pl.pallas_call(x_kernel, out_shape=[jax.ShapeDtypeStruct((XR, 2, 3, piece...  27.9 us
    ppermute x2, waiting for transfers between devices, lines_local(): got.append(lax.ppermute(part, 'gz', swap))  24.4 us
    ppermute x2, waiting for transfers between devices, lines_local(): got_terms.append(lax.ppermute(other, 'gz', swap))  18.6 us
    unnamed x28, local copies, waits for them, and re-layouts  18.2 us
    pallas_call x2, Pallas kernels, lines_local(): pl.pallas_call(z_forward_kernel, out_shape=[jax.ShapeDtypeStruct((4, piec...  11.7 us
    pallas_call x2, Pallas kernels, lines_local(): pl.pallas_call(z_inverse_kernel, out_shape=jax.ShapeDtypeStruct((ZR, 4, 2...  10.3 us
    pallas_call x1, Pallas kernels, lines_local(): pl.pallas_call(advance_kernel, grid=(mode_count // block,), out_shape=[ja...  8.61 us
  transfers between devices with their start and end apart: 4, of which 2 were waited for; matrix products, arithmetic and copies ran while one was open for 0% of the time, Pallas kernels for 35%

commit v1 on v0

--- a/solution.py
+++ b/solution.py
@@ -208,7 +208,13 @@
 LOW = (0, 1, 2)
 HIGH = (5, 6, 7)
 MIB = 1 << 20
-PIECES = 2
+CHUNKS = 4
+UNIT = 8
+UNITS = 11
+SIDE = 16 * UNITS
+SKIP = NX // UNIT - 2 * SIDE
+SPANS = 4
+LARGE = 3
 
 
 def split_table(table):
@@ -287,17 +293,15 @@
     )
 
 
-def z_inverse_kernel(half_ref, own_ref, other_ref, high_ref, low_ref, out_ref, th_ref, tl_ref):
-    rows = own_ref.shape[2]
+def z_inverse(first, own_ref, other_ref, row, rows, high_ref, low_ref, out_ref, th_ref, tl_ref):
     step = 16
-    first = half_ref[0] == 0
     for c in range(2):
         def body(i, carry):
             at = pl.multiple_of(i * step, step)
             for lane in range(0, ZS, 128):
                 values = [None] * ZR
                 for a in range(ZR // 2):
-                    to = (pl.ds(at, step), pl.ds(a * ZS + lane, 128))
+                    to = (pl.ds(row + at, step), pl.ds(a * ZS + lane, 128))
                     own = [own_ref[(c, p) + to] for p in range(2)]
                     other = [other_ref[(c, p) + to] for p in range(2)]
                     values[a] = tuple(jnp.where(first, x, y) for x, y in zip(own, other))
@@ -322,34 +326,31 @@
             for t in range(2):
                 at = p * ZS + t * 128
                 even, odd = merge(done[:rows, at : at + 128], done[rows:, at : at + 128], low_half)
-                out_ref[r, 2 * t, p] = even
-                out_ref[r, 2 * t + 1, p] = odd
+                out_ref[r * 4 + 2 * t, p, pl.ds(row, rows), :] = even
+                out_ref[r * 4 + 2 * t + 1, p, pl.ds(row, rows), :] = odd
         return carry
     lax.fori_loop(0, ZR, group, 0)
 
 
-def x_kernel(*refs):
-    v_refs, (ih_ref, il_ref, fh_ref, fl_ref) = refs[:PIECES], refs[PIECES : PIECES + 4]
-    out_refs = refs[PIECES + 4 : 2 * PIECES + 4]
-    th_ref, tl_ref, u_ref = refs[2 * PIECES + 4 :]
-    rows = v_refs[0].shape[3]
+def x_spread(v_ref, row, rows, th_ref, tl_ref):
     step = 16
-    for r, h in ((r, h) for r in range(2) for h in range(PIECES)):
-        v_ref, base = v_refs[h], (r * PIECES + h) * rows
-
+    half = XS // 2
+    for r in range(2):
         def body(i, carry):
-            at = pl.multiple_of(i * step, step)
+            at = pl.multiple_of(row + i * step, step)
             values = [
-                tuple(v_ref[g, r, p, pl.ds(at, step), :] for p in range(2)) for g in range(XR)
+                tuple(v_ref[2 * g + r, p, pl.ds(at, step), :] for p in range(2)) for g in range(XR)
             ]
             for res, pair in enumerate(small_dft(values, 1)):
                 for p in range(2):
                     high, low = parts_of(pair[p])
-                    th_ref[res, pl.ds(p * XS + base + at, step), :] = high
-                    tl_ref[res, pl.ds(p * XS + base + at, step), :] = low
+                    th_ref[res, pl.ds(p * XS + r * half + at, step), :] = high
+                    tl_ref[res, pl.ds(p * XS + r * half + at, step), :] = low
             return carry
         lax.fori_loop(0, rows // step, body, 0)
 
+
+def x_products(ih_ref, il_ref, fh_ref, fl_ref, th_ref, tl_ref, u_ref):
     def residue(res, carry):
         field = dot3(ih_ref[res], il_ref[res], th_ref[res], tl_ref[res], ((1,), (0,)))
         swapped = pltpu.roll(field, 64, 1)
@@ -359,37 +360,51 @@
         return carry
     lax.fori_loop(0, XR, residue, 0)
 
-    low_half = lax.broadcasted_iota(jnp.int32, (8, 128), 1) < 64
-    for r, n in ((r, n) for r in range(2) for n in range(PIECES)):
-        out_ref, base = out_refs[n], (r * PIECES + n) * rows
-
+
+def x_gather(u_ref, out_ref):
+    low_half = lax.broadcasted_iota(jnp.int32, (UNIT, 128), 1) < 64
+    per = XS // UNIT
+    split = SIDE % per
+    for first, last in ((0, split), (split, per)):
         def back(i, carry):
-            at = pl.multiple_of(i * 8, 8)
+            at = pl.multiple_of(i * UNIT, UNIT)
             for h in range(2):
                 values = [
                     tuple(
-                        u_ref[res, pl.ds(p * XS + base + at, 8), pl.ds(h * 128, 128)]
+                        u_ref[res, pl.ds(p * XS + at, UNIT), pl.ds(h * 128, 128)]
                         for p in range(2)
                     )
                     for res in range(XR)
                 ]
                 for g, (re, im) in enumerate(small_dft(values, -1)):
+                    if g * per + first < SIDE:
+                        flat = g * per + i
+                    elif g * per + first >= SIDE + SKIP:
+                        flat = g * per + i - SKIP
+                    else:
+                        continue
+                    worker = flat // UNITS
+                    line = pl.ds(pl.multiple_of((flat - worker * UNITS) * UNIT, UNIT), UNIT)
                     if h == 0:
-                        out_ref[g, r, 0, pl.ds(at, 8), :] = re
-                        out_ref[g, r, 1, pl.ds(at, 8), :] = im
+                        out_ref[worker, 0, line, :] = re
+                        out_ref[worker, 1, line, :] = im
                     else:
-                        out_ref[g, r, 2, pl.ds(at, 8), :] = jnp.where(low_half, re, im)
+                        out_ref[worker, 2, line, :] = jnp.where(low_half, re, im)
             return carry
-        lax.fori_loop(0, rows // 8, back, 0)
-
-
-def z_forward_kernel(half_ref, v_ref, high_ref, low_ref, wave_ref, keep_ref, own_ref, other_ref, w_ref):
-    lower = half_ref[0] == 0
-    rows = v_ref.shape[3]
+        lax.fori_loop(first, last, back, 0)
+
+
+def unit_of(flat):
+    return jnp.where(flat < SIDE, flat, flat + SKIP)
+
+
+def z_forward(first_unit, row, rows, v_ref, high_ref, low_ref, out_ref, w_ref):
     low_half = lax.broadcasted_iota(jnp.int32, (rows, 128), 1) < 64
 
     def group(r, carry):
-        real, imag, mixed = ([v_ref[r, j, x] for j in range(4)] for x in range(3))
+        real, imag, mixed = (
+            [v_ref[r * 4 + j, x, pl.ds(row, rows), :] for j in range(4)] for x in range(3)
+        )
         p0r, p2r, p0i, p2i, p1r, p1i = [], [], [], [], [], []
         for source, first, second in ((real, p0r, p2r), (imag, p0i, p2i), (mixed, p1r, p1i)):
             for t in range(2):
@@ -404,71 +419,303 @@
             dot3(high, low, high_ref[r, :, at : at + ZS], low_ref[r, :, at : at + ZS], ((1,), (1,)))
             for at in (0, ZS)
         )
-        w_ref[r, :, :ZS] = cos[: 3 * rows] + sin[3 * rows :]
-        w_ref[r, :, ZS:] = cos[3 * rows :] - sin[: 3 * rows]
+        w_ref[r, : 3 * rows, :ZS] = cos[: 3 * rows] + sin[3 * rows :]
+        w_ref[r, : 3 * rows, ZS:] = cos[3 * rows :] - sin[: 3 * rows]
         return carry
     lax.fori_loop(0, ZR, group, 0)
 
     def body(i, carry):
-        at = pl.multiple_of(i * 8, 8)
-        wave_along = wave_ref[pl.ds(at, 8), :]
-        keep_along = keep_ref[pl.ds(at, 8), :]
+        at = pl.multiple_of(i * UNIT, UNIT)
+        along = unit_of(first_unit + i) * UNIT + lax.broadcasted_iota(jnp.int32, (UNIT, 128), 0)
+        along = jnp.where(2 * along < NX, along, along - NX)
+        wave_along = along.astype(jnp.float32) * (TWO_PI / NX)
+        keep_along = 3 * jnp.abs(along) < NX
         for lane in range(0, ZS, 128):
             spectra = []
             for j in range(3):
                 values = [
                     tuple(
-                        w_ref[r, pl.ds(j * rows + at, 8), pl.ds(p * ZS + lane, 128)]
+                        w_ref[r, pl.ds(j * rows + at, UNIT), pl.ds(p * ZS + lane, 128)]
                         for p in range(2)
                     )
                     for r in range(ZR)
                 ]
                 spectra.append(small_dft(values, -1))
-            for place in range(len(LOW)):
-                terms = []
-                for half, groups in enumerate((LOW, HIGH)):
-                    a = groups[place]
+            for half, groups in enumerate((LOW, HIGH)):
+                for place, a in enumerate(groups):
                     start = a * ZS + lane - (NZ if half else 0)
-                    mode = start + lax.broadcasted_iota(jnp.int32, (8, 128), 1)
+                    mode = start + lax.broadcasted_iota(jnp.int32, (UNIT, 128), 1)
                     wave_across = mode.astype(jnp.float32) * (TWO_PI / NZ)
-                    keep = jnp.logical_and(3 * jnp.abs(mode) < NZ, keep_along > 0.5)
+                    keep = jnp.logical_and(3 * jnp.abs(mode) < NZ, keep_along)
                     (ar, ai), (br, bi), (cr, ci) = (x[a] for x in spectra)
-                    terms.append(
-                        [
-                            jnp.where(keep, wave_along * ai + wave_across * bi, 0.0),
-                            jnp.where(keep, -(wave_along * ar + wave_across * br), 0.0),
-                            jnp.where(keep, wave_along * bi + wave_across * ci, 0.0),
-                            jnp.where(keep, -(wave_along * br + wave_across * cr), 0.0),
-                        ]
-                    )
-                to = (pl.ds(at, 8), pl.ds(place * ZS + lane, 128))
-                for x in range(4):
-                    own_ref[(x,) + to] = jnp.where(lower, terms[0][x], terms[1][x])
-                    other_ref[(x,) + to] = jnp.where(lower, terms[1][x], terms[0][x])
-        return carry
-    lax.fori_loop(0, rows // 8, body, 0)
-
-
-def advance_kernel(half_ref, base_ref, v_ref, old_ref, *refs):
-    own_refs, got_refs = refs[:PIECES], refs[PIECES : 2 * PIECES]
-    along_ref, across_ref, next_ref, non_ref = refs[2 * PIECES :]
-    place = pl.program_id(0)
-    is_own = place // PIECES == half_ref[0]
-    piece = lax.rem(place, PIECES)
+                    terms = [
+                        jnp.where(keep, wave_along * ai + wave_across * bi, 0.0),
+                        jnp.where(keep, -(wave_along * ar + wave_across * br), 0.0),
+                        jnp.where(keep, wave_along * bi + wave_across * ci, 0.0),
+                        jnp.where(keep, -(wave_along * br + wave_across * cr), 0.0),
+                    ]
+                    for x in range(4):
+                        out_ref[half, x, pl.ds(row + at, UNIT), pl.ds(place * ZS + lane, 128)] = terms[x]
+        return carry
+    lax.fori_loop(0, rows // UNIT, body, 0)
+
+
+def substep_kernel(
+    velocity_ref, zh_hbm, zl_hbm, ih_hbm, il_hbm, fh_hbm, fl_hbm,
+    term_ref,
+    own_ref, other_ref, zh_ref, zl_ref, ih_ref, il_ref, fh_ref, fl_ref,
+    zth_ref, ztl_ref, out_ref, in_ref, th_ref, tl_ref, u_ref, back_ref, work_ref, w_ref, res_ref,
+    table_sems, own_sems, swap_send, swap_recv, out_send, out_recv, back_send, back_recv,
+    res_send, res_recv,
+):
+    gx, gz = lax.axis_index("gx"), lax.axis_index("gz")
+    count = 2 * XR
+    me = 2 * gx + gz
+    half = own_ref.shape[2]
+    rows = half // CHUNKS
+
+    def device(t):
+        return (t // 2, lax.rem(t, 2))
+
+    tables = [
+        pltpu.make_async_copy(src, dst, table_sems.at[n])
+        for n, (src, dst) in enumerate(
+            (
+                (zh_hbm, zh_ref),
+                (zl_hbm, zl_ref),
+                (ih_hbm, ih_ref),
+                (il_hbm, il_ref),
+                (fh_hbm, fh_ref),
+                (fl_hbm, fl_ref),
+            )
+        )
+    ]
+
+    def load_own(c):
+        return pltpu.make_async_copy(
+            velocity_ref.at[:, :, pl.ds(pl.multiple_of(gz * half + c * rows, rows), rows), :],
+            own_ref.at[:, :, pl.ds(pl.multiple_of(c * rows, rows), rows), :],
+            own_sems.at[c],
+        )
+
+    def swap(c):
+        return pltpu.make_async_remote_copy(
+            src_ref=velocity_ref.at[
+                :, :, pl.ds(pl.multiple_of((1 - gz) * half + c * rows, rows), rows), :
+            ],
+            dst_ref=other_ref.at[:, :, pl.ds(pl.multiple_of(c * rows, rows), rows), :],
+            send_sem=swap_send.at[c],
+            recv_sem=swap_recv.at[c],
+            device_id=(gx, 1 - gz),
+            device_id_type=pl.DeviceIdType.MESH,
+        )
+
+    for c in range(CHUNKS):
+        load_own(c).start()
+    for table in tables:
+        table.start()
+
+    barrier = pltpu.get_barrier_semaphore()
+
+    def greet(i, carry):
+        pl.semaphore_signal(
+            barrier,
+            inc=1,
+            device_id=device(lax.rem(me + i, count)),
+            device_id_type=pl.DeviceIdType.MESH,
+        )
+        return carry
+
+    lax.fori_loop(1, count, greet, 0)
+    pl.semaphore_wait(barrier, count - 1)
+    for c in range(CHUNKS):
+        swap(c).start()
+
+    def ship(src_ref, dst_ref, sends, recvs, c, at, length):
+        span = pl.ds(at, length)
+
+        def copy(i):
+            t = lax.rem(me + i, count)
+            return pltpu.make_async_remote_copy(
+                src_ref=src_ref.at[t, :, span, :],
+                dst_ref=dst_ref.at[me, :, span, :],
+                send_sem=sends.at[c, i],
+                recv_sem=recvs.at[c, i],
+                device_id=device(t),
+                device_id_type=pl.DeviceIdType.MESH,
+            )
+
+        local = pltpu.make_async_copy(
+            src_ref.at[me, :, span, :], dst_ref.at[me, :, span, :], recvs.at[c, 0]
+        )
+        return copy, local
+
+    def ship_start(*args):
+        copy, local = ship(*args)
+
+        def start(i, carry):
+            copy(i).start()
+            return carry
+
+        lax.fori_loop(1, count, start, 0)
+        local.start()
+
+    def ship_arrive(*args):
+        copy, local = ship(*args)
+
+        def wait(i, carry):
+            copy(i).wait_recv()
+            return carry
+
+        lax.fori_loop(1, count, wait, 0)
+        local.wait()
+
+    def ship_leave(*args):
+        copy, _ = ship(*args)
+
+        def wait(i, carry):
+            copy(i).wait_send()
+            return carry
+
+        lax.fori_loop(1, count, wait, 0)
+
+    def spread_args(c):
+        return out_ref, in_ref, out_send, out_recv, c, pl.multiple_of(c * rows, rows), rows
+
+    tables[0].wait()
+    tables[1].wait()
+
+    def inverse(c, carry):
+        load_own(c).wait()
+        swap(c).wait_recv()
+        z_inverse(
+            gz == 0, own_ref, other_ref, pl.multiple_of(c * rows, rows), rows,
+            zh_ref, zl_ref, out_ref, zth_ref, ztl_ref,
+        )
+        ship_start(*spread_args(c))
+        return carry
+
+    lax.fori_loop(0, CHUNKS, inverse, 0)
+
+    def spread(c, carry):
+        ship_arrive(*spread_args(c))
+        x_spread(in_ref, pl.multiple_of(c * rows, rows), rows, th_ref, tl_ref)
+        return carry
+
+    lax.fori_loop(0, CHUNKS, spread, 0)
+    for table in tables[2:]:
+        table.wait()
+    x_products(ih_ref, il_ref, fh_ref, fl_ref, th_ref, tl_ref, u_ref)
+    x_gather(u_ref, back_ref)
+
+    def back_args(c, units):
+        at = pl.multiple_of(c * LARGE * UNIT, UNIT)
+        return back_ref, work_ref, back_send, back_recv, c, at, units * UNIT
+
+    last = UNITS - LARGE * (SPANS - 1)
+
+    def over_spans(step):
+        def one(c, carry):
+            step(c, LARGE)
+            return carry
+
+        lax.fori_loop(0, SPANS - 1, one, 0)
+        step(SPANS - 1, last)
+
+    over_spans(lambda c, units: ship_start(*back_args(c, units)))
+
+    per = XS // UNIT
+
+    def result(u, side):
+        unit = unit_of(UNITS * me + u)
+        owner = unit // per
+        slot = unit - owner * per
+        src = res_ref.at[side, :, pl.ds(pl.multiple_of(u * UNIT, UNIT), UNIT), :]
+        dst = term_ref.at[:, pl.ds(pl.multiple_of(slot * UNIT, UNIT), UNIT), :]
+        here = jnp.logical_and(owner == gx, side == gz)
+        remote = pltpu.make_async_remote_copy(
+            src_ref=src,
+            dst_ref=dst,
+            send_sem=res_send.at[side, u],
+            recv_sem=res_recv.at[slot],
+            device_id=(owner, side),
+            device_id_type=pl.DeviceIdType.MESH,
+        )
+        return here, remote, pltpu.make_async_copy(src, dst, res_recv.at[slot])
+
+    def forward(c, units):
+        ship_arrive(*back_args(c, units))
+        unit = c * LARGE
+        z_forward(
+            UNITS * me + unit, pl.multiple_of(unit * UNIT, UNIT), units * UNIT,
+            work_ref, zh_ref, zl_ref, res_ref, w_ref,
+        )
+
+        def send(n, carry):
+            for side in range(2):
+                here, remote, local = result(unit + n, side)
+
+                @pl.when(here)
+                def _():
+                    local.start()
+
+                @pl.when(jnp.logical_not(here))
+                def _():
+                    remote.start()
+            return carry
+
+        lax.fori_loop(0, units, send, 0)
+
+    over_spans(forward)
+
+    def sent(u, carry):
+        for side in range(2):
+            here, remote, _ = result(u, side)
+
+            @pl.when(jnp.logical_not(here))
+            def _():
+                remote.wait_send()
+        return carry
+
+    def got(s, carry):
+        unit = gx * per + s
+
+        @pl.when(jnp.logical_or(unit < SIDE, unit >= SIDE + SKIP))
+        def _():
+            pltpu.make_async_copy(
+                res_ref.at[0, :, pl.ds(0, UNIT), :],
+                term_ref.at[:, pl.ds(pl.multiple_of(s * UNIT, UNIT), UNIT), :],
+                res_recv.at[s],
+            ).wait()
+        return carry
+
+    lax.fori_loop(0, per, got, 0)
+    lax.fori_loop(0, UNITS, sent, 0)
+
+    def swap_left(c, carry):
+        swap(c).wait_send()
+        ship_leave(*spread_args(c))
+        return carry
+
+    lax.fori_loop(0, CHUNKS, swap_left, 0)
+    over_spans(lambda c, units: ship_leave(*back_args(c, units)))
+
+
+def advance_kernel(place_ref, base_ref, v_ref, old_ref, term_ref, along_ref, across_ref, next_ref, non_ref):
     rows, extent = v_ref.shape[2:]
+    unit = place_ref[0] * (XS // UNIT) + pl.program_id(0) * (rows // UNIT)
+    lower = place_ref[1] == 0
+    active = jnp.logical_or(unit < SIDE, unit >= SIDE + SKIP)
     wave_along = along_ref[:, :1]
     wave_across = across_ref[:1, :]
     damping = jnp.exp(-VISCOSITY * (wave_along * wave_along + wave_across * wave_across))
     shear = base_ref[0] * wave_along
-    empty = jnp.zeros((rows, extent - own_refs[0].shape[2]), jnp.float32)
+    empty = jnp.zeros((rows, extent - term_ref.shape[2]), jnp.float32)
     for c in range(2):
         for p in range(2):
-            term = None
-            for h in range(PIECES):
-                this = jnp.where(is_own, own_refs[h][2 * c + p], got_refs[h][2 * c + p])
-                term = this if term is None else jnp.where(piece == h, this, term)
+            term = jnp.where(active, term_ref[2 * c + p], 0.0)
             term = jnp.where(
-                half_ref[0] == 0,
+                lower,
                 jnp.concatenate([term, empty], axis=1),
                 jnp.concatenate([empty, term], axis=1),
             )
@@ -480,174 +727,73 @@
             )
 
 
-def whole(*_):
-    return pl.BlockSpec(memory_space=pltpu.VMEM)
-
-
-def params(limit):
-    return pltpu.CompilerParams(vmem_limit_bytes=limit * MIB)
-
-
-def kept(block, block_rows):
-    start = block * block_rows
-    return jnp.logical_or(3 * start < NX, 3 * (NX - start - block_rows + 1) < NX)
-
-
-def exchange_kernel(block_rows, src_ref, dst_ref, send_sems, recv_sems, own_sem):
-    across = lax.axis_size("gz")
-    count = lax.axis_size("gx") * across
-    me = lax.axis_index("gx") * across + lax.axis_index("gz")
-
-    def device(t):
-        return (t // across, lax.rem(t, across))
-
-    def wanted(t):
-        return kept(t, block_rows) if block_rows else t >= 0
-
-    barrier = pltpu.get_barrier_semaphore()
-
-    def greet(i, carry):
-        pl.semaphore_signal(
-            barrier,
-            inc=1,
-            device_id=device(lax.rem(me + i, count)),
-            device_id_type=pl.DeviceIdType.MESH,
-        )
-        return carry
-
-    lax.fori_loop(1, count, greet, 0)
-    pl.semaphore_wait(barrier, count - 1)
-
-    def copy(i):
-        t = lax.rem(me + i, count)
-        return pltpu.make_async_remote_copy(
-            src_ref=src_ref.at[t],
-            dst_ref=dst_ref.at[me],
-            send_sem=send_sems.at[i],
-            recv_sem=recv_sems.at[i],
-            device_id=device(t),
-            device_id_type=pl.DeviceIdType.MESH,
-        )
-
-    def start(i, carry):
-        @pl.when(wanted(lax.rem(me + i, count)))
-        def _():
-            copy(i).start()
-
-        return carry
-
-    lax.fori_loop(1, count, start, 0)
-    own = pltpu.make_async_copy(src_ref.at[me], dst_ref.at[me], own_sem)
-    own.start()
-    own.wait()
-
-    def finish(i, carry):
-        @pl.when(wanted(lax.rem(me + i, count)))
-        def _():
-            copy(i).wait_send()
-
-        @pl.when(wanted(me))
-        def _():
-            copy(i).wait_recv()
-
-        return carry
-
-    lax.fori_loop(1, count, finish, 0)
-
-
-def exchange(value, number, block_rows=0):
-    count = value.shape[0]
-    return pl.pallas_call(
-        functools.partial(exchange_kernel, block_rows),
-        out_shape=jax.ShapeDtypeStruct(value.shape, value.dtype),
-        in_specs=[pl.BlockSpec(memory_space=pl.ANY)],
-        out_specs=pl.BlockSpec(memory_space=pl.ANY),
-        scratch_shapes=[
-            pltpu.SemaphoreType.DMA((count,)),
-            pltpu.SemaphoreType.DMA((count,)),
-            pltpu.SemaphoreType.DMA,
-        ],
-        compiler_params=pltpu.CompilerParams(collective_id=number, has_side_effects=True),
-        cost_estimate=pl.CostEstimate(flops=0, bytes_accessed=64 * value.size, transcendentals=0),
-        name="exchange_" + str(number),
-    )(value)
-
-
 def lines_local(velocity, previous, base_flow):
     velocity, previous = velocity[:, :, 0], previous[:, :, 0]
     mode_count, extent = velocity.shape[2:]
-    rows = mode_count // 2
+    half = mode_count // 2
+    rows = half // CHUNKS
     gx, gz = lax.axis_index("gx"), lax.axis_index("gz")
     f32, bf16 = jnp.float32, jnp.bfloat16
     zh, zl = z_table()
     xh, xl = x_table()
     fh, fl = np.swapaxes(xh, 1, 2), np.swapaxes(xl, 1, 2)
-
-    piece = rows // PIECES
-    half = gz.astype(jnp.int32)[None]
-    scalar = pl.BlockSpec(memory_space=pltpu.SMEM)
-    swap = [(0, 1), (1, 0)]
-    got, swapped = [], []
-    for h in range(PIECES):
-        part = lax.dynamic_slice_in_dim(velocity, (1 - gz) * rows + h * piece, piece, axis=2)
-        if h:
-            part, got[h - 1] = lax.optimization_barrier((part, got[h - 1]))
-        got.append(lax.ppermute(part, "gz", swap))
-    for h in range(PIECES):
-        mine = lax.dynamic_slice_in_dim(velocity, gz * rows + h * piece, piece, axis=2)
-        if h:
-            mine, swapped[h - 1] = lax.optimization_barrier((mine, swapped[h - 1]))
-        along_z = pl.pallas_call(
-            z_inverse_kernel,
-            out_shape=jax.ShapeDtypeStruct((ZR, 4, 2, piece, 128), f32),
-            in_specs=[scalar] + [whole()] * 4,
-            out_specs=whole(),
-            scratch_shapes=[pltpu.VMEM((ZR, 4 * piece, ZS), bf16)] * 2,
-            compiler_params=params(40),
-            name="z_inverse",
-        )(half, mine, got[h], zh, zl)
-        swapped.append(exchange(along_z.reshape(32, 2, piece, 128), 1 + h))
-    worked = pl.pallas_call(
-        x_kernel,
-        out_shape=[jax.ShapeDtypeStruct((XR, 2, 3, piece, 128), f32)] * PIECES,
-        in_specs=[whole()] * (PIECES + 4),
-        out_specs=[whole()] * PIECES,
-        scratch_shapes=[pltpu.VMEM((XR, 2 * XS, 128), bf16)] * 2
-        + [pltpu.VMEM((XR, 2 * XS, 256), f32)],
-        compiler_params=params(56),
-        name="x_work",
-    )(*(x.reshape(XR, 2, 2, piece, 128) for x in swapped), xh, xl, fh, fl)
+    active = len(LOW) * ZS
+    count = 2 * XR
+    dma = pltpu.SemaphoreType.DMA
+
+    term = pl.pallas_call(
+        substep_kernel,
+        out_shape=jax.ShapeDtypeStruct((4, mode_count, active), f32),
+        in_specs=[pl.BlockSpec(memory_space=pl.ANY)] * 7,
+        out_specs=pl.BlockSpec(memory_space=pl.ANY),
+        scratch_shapes=[
+            pltpu.VMEM((2, 2, half, extent), f32),
+            pltpu.VMEM((2, 2, half, extent), f32),
+            pltpu.VMEM(zh.shape, bf16),
+            pltpu.VMEM(zl.shape, bf16),
+            pltpu.VMEM(xh.shape, bf16),
+            pltpu.VMEM(xl.shape, bf16),
+            pltpu.VMEM(fh.shape, bf16),
+            pltpu.VMEM(fl.shape, bf16),
+            pltpu.VMEM((ZR, 4 * rows, ZS), bf16),
+            pltpu.VMEM((ZR, 4 * rows, ZS), bf16),
+            pltpu.VMEM((count, 2, half, 128), f32),
+            pltpu.VMEM((count, 2, half, 128), f32),
+            pltpu.VMEM((XR, 2 * XS, 128), bf16),
+            pltpu.VMEM((XR, 2 * XS, 128), bf16),
+            pltpu.VMEM((XR, 2 * XS, 256), f32),
+            pltpu.VMEM((count, 3, UNITS * UNIT, 128), f32),
+            pltpu.VMEM((count, 3, UNITS * UNIT, 128), f32),
+            pltpu.VMEM((ZR, 3 * LARGE * UNIT, 2 * ZS), f32),
+            pltpu.VMEM((2, 4, UNITS * UNIT, active), f32),
+            dma((6,)),
+            dma((CHUNKS,)),
+            dma((CHUNKS,)),
+            dma((CHUNKS,)),
+            dma((CHUNKS, count)),
+            dma((CHUNKS, count)),
+            dma((SPANS, count)),
+            dma((SPANS, count)),
+            dma((2, UNITS)),
+            dma((XS // UNIT,)),
+        ],
+        compiler_params=pltpu.CompilerParams(
+            collective_id=1, has_side_effects=True, vmem_limit_bytes=60 * MIB
+        ),
+        cost_estimate=pl.CostEstimate(
+            flops=10**10, bytes_accessed=64 * velocity.size, transcendentals=0
+        ),
+        name="substep",
+    )(velocity, zh, zl, xh, xl, fh, fl)
 
     def modes(start, count, size):
         numbers = start + jnp.arange(count, dtype=jnp.int32)
         return jnp.where(2 * numbers < size, numbers, numbers - size)
 
-    own = modes(gx * mode_count + gz * rows, rows, NX)[:, None]
-    own_wave = jnp.broadcast_to(own.astype(f32) * (TWO_PI / NX), (rows, 128))
-    own_keep = jnp.broadcast_to((3 * jnp.abs(own) < NX).astype(f32), (rows, 128))
-    active = len(LOW) * ZS
-    own_terms, got_terms = [], []
-    for h in range(PIECES):
-        sent = worked[h].reshape(32, 3, piece, 128)
-        if h:
-            sent, own_terms[h - 1] = lax.optimization_barrier((sent, own_terms[h - 1]))
-        returned = exchange(sent, 1 + PIECES + h, rows)
-        at = slice(h * piece, (h + 1) * piece)
-        mine, other = pl.pallas_call(
-            z_forward_kernel,
-            out_shape=[jax.ShapeDtypeStruct((4, piece, active), f32)] * 2,
-            in_specs=[scalar] + [whole()] * 5,
-            out_specs=[whole()] * 2,
-            scratch_shapes=[pltpu.VMEM((ZR, 3 * piece, 2 * ZS), f32)],
-            compiler_params=params(40),
-            name="z_forward",
-        )(half, returned.reshape(ZR, 4, 3, piece, 128), zh, zl, own_wave[at], own_keep[at])
-        own_terms.append(mine)
-        got_terms.append(lax.ppermute(other, "gz", swap))
-
     along = modes(gx * mode_count, mode_count, NX).astype(f32) * (TWO_PI / NX)
     across = modes(gz * extent, extent, NZ).astype(f32) * (TWO_PI / NZ)
-    block = piece
+    scalar = pl.BlockSpec(memory_space=pltpu.SMEM)
+    block = 64
     field = pl.BlockSpec((2, 2, block, extent), lambda i: (0, 0, i, 0))
     advanced, nonlinear = pl.pallas_call(
         advance_kernel,
@@ -658,20 +804,19 @@
             scalar,
             field,
             field,
-            *([pl.BlockSpec((4, block, active), lambda i: (0, 0, 0))] * (2 * PIECES)),
+            pl.BlockSpec((4, block, active), lambda i: (0, i, 0)),
             pl.BlockSpec((block, 128), lambda i: (i, 0)),
             pl.BlockSpec((8, extent), lambda i: (0, 0)),
         ],
         out_specs=[field, field],
-        compiler_params=params(48),
+        compiler_params=pltpu.CompilerParams(vmem_limit_bytes=48 * MIB),
         name="advance",
     )(
-        half,
+        jnp.stack([gx, gz]).astype(jnp.int32),
         base_flow,
         velocity,
         previous,
-        *own_terms,
-        *got_terms,
+        term,
         jnp.broadcast_to(along[:, None], (mode_count, 128)),
         jnp.broadcast_to(across[None], (8, extent)),
     )

time: 351 us -> 266 us (0.76)
  waiting for transfers between devices: 43 us -> 0 us
  local copies, waits for them, and re-layouts: 22.9 us -> 1.98 us
  Pallas kernels: 282 us -> 262 us
    ppermute x4 -> x0, waiting for transfers between devices: 43 us -> none  [the longest x2 24.4 us: lines_local(): got.append(lax.ppermute(part, 'gz', swap))]
    pallas_call x9 -> x1, Pallas kernels: 273 us -> 254 us  [lines_local(): pl.pallas_call(substep_kernel, out_shape=jax.ShapeDtypeStruct((4, mode_co...]
    unnamed x28 -> x2, local copies, waits for them, and re-layouts: 18.2 us -> 1.88 us
    dynamic_slice x1 -> x0, local copies, waits for them, and re-layouts: 4.1 us -> none  [lines_local(): lax.dynamic_slice_in_dim(velocity, (1 - gz) * rows + h * piece, piece, ax...]
  transfers between devices with their start and end apart: 4 -> 0, of which waited for: 2 -> 0; matrix products, arithmetic and copies ran while one was open for 0% -> 0% of each run, Pallas kernels for 35% -> 0%
where the time goes in v1:
time: 266 us
  Pallas kernels  262 us (98%)
    pallas_call x1, Pallas kernels, lines_local(): pl.pallas_call(substep_kernel, out_shape=jax.ShapeDtypeStruct((4, mode_co...  254 us
    pallas_call x1, Pallas kernels, lines_local(): pl.pallas_call(advance_kernel, grid=(mode_count // block,), out_shape=[ja...  7.99 us

profile of v1, /device:TPU:12, one launch (start us, length us, event | category | flops | bytes accessed | tf_op | source)
XLA Modules:
  0.0 265.7 jit_solution(9680609270069634780)
XLA Ops:
  1.3 0.1 pad_add_fusion.place_ref
  1.4 0.1 broadcast_in_dim.8.along_ref
  1.5 254.4 %substep.1.term_ref = f32[4,256,768]{2,1,0:T(8,128)} custom-call(f32[2,2,256,1024]{3,2,1,0:T(8,128)} %bitcast.10, bf16[8,256,512]{2,1,0:T(8,128)(2,1)} %constant.39.clone.zh_hbm, bf16[8,256,512]{2,1,0:T(8,128)(2,1)} %constant.40.clone.zl_hbm, bf16[16,256,512]{2,1,0:T(8,128)(2,1)} %constant.41.clone.ih_hbm, bf16[16,256,512]{2,1,0:T(8,128)(2,1)} %constant.42.clone.il_hbm, ...), custom_call_target="tpu_custom_call" | custom-call | flops 10000000000 | bytes 67108864 | tf_op jit(solution)/shard_map/substep/pallas_call | solution.py:744
  255.9 0.0 copy-start
  255.9 1.9 copy-done
  257.8 8.0 %advance.1 = (f32[2,2,256,1024]{3,2,1,0:T(8,128)}, f32[2,2,256,1024]{3,2,1,0:T(8,128)}) custom-call(s32[2]{0:T(128)S(1)} %pad_add_fusion.place_ref, f32[1]{0:T(128)S(6)} %copy.13.base_ref, f32[2,2,256,1024]{3,2,1,0:T(8,128)} %bitcast.11, f32[2,2,256,1024]{3,2,1,0:T(8,128)} %bitcast.12, f32[4,256,768]{2,1,0:T(8,128)S(1)} %copy-done, ...), custom_call_target="tpu_custom_call" | custom-call | tf_op jit(solution)/shard_map/advance/pallas_call | solution.py:798
  (3 shorter events, 0.0 us)
Async XLA Ops:
  255.9 1.9 copy-start

commit v2 on v1

--- a/solution.py
+++ b/solution.py
@@ -208,13 +208,16 @@
 LOW = (0, 1, 2)
 HIGH = (5, 6, 7)
 MIB = 1 << 20
-CHUNKS = 4
+CHUNKS = (16, 16, 32, 32, 32)
 UNIT = 8
 UNITS = 11
 SIDE = 16 * UNITS
-SKIP = NX // UNIT - 2 * SIDE
-SPANS = 4
-LARGE = 3
+PER = XS // UNIT
+OWN = 2 * UNITS
+EXTRA = PER - OWN
+SPANS = (2, 2, 2, 2, 2, 1)
+BACK_AHEAD = 6
+UNROLL = 16
 
 
 def split_table(table):
@@ -316,7 +319,9 @@
         lax.fori_loop(0, rows // step, body, 0)
 
     def group(r, carry):
-        both = dot3(th_ref[r], tl_ref[r], high_ref[r], low_ref[r], ((1,), (0,)))
+        both = dot3(
+            th_ref[r, : 4 * rows], tl_ref[r, : 4 * rows], high_ref[r], low_ref[r], ((1,), (0,))
+        )
         real, imag = both[: 2 * rows], both[2 * rows :]
         done = jnp.concatenate(
             [real[:, :ZS] - imag[:, ZS:], real[:, ZS:] + imag[:, :ZS]], axis=1
@@ -358,14 +363,49 @@
         high, low = parts_of(products)
         u_ref[res] = dot3(fh_ref[res], fl_ref[res], high, low, ((1,), (0,)))
         return carry
-    lax.fori_loop(0, XR, residue, 0)
+    lax.fori_loop(0, XR, residue, 0, unroll=UNROLL)
+
+
+def place_of(o, s):
+    e = s - OWN
+    if o < 2:
+        e = e + o * EXTRA
+        m = jnp.where(s < OWN, o, jnp.where(e < 14, 4, 5))
+        n = jnp.where(s < OWN, s, jnp.where(e < 14, e, e - 14))
+    elif o < 4:
+        e = e + (o - 2) * EXTRA
+        m = jnp.where(s < OWN, o, 6 + lax.rem(e, 2))
+        n = jnp.where(s < OWN, s, e // 2)
+    elif o == 4:
+        e = s + 12
+        m = jnp.where(s < 8, 4, 6 + lax.rem(e, 2))
+        n = jnp.where(s < 8, s + 14, e // 2)
+    else:
+        m, n = 5, s + 6
+    return m, lax.rem(n, 2), n // 2
+
+
+def unit_at(gx, gz, u):
+    right = gx >= XR // 2
+    m = jnp.where(right, XR - 1 - gx, gx)
+    n = 2 * u + gz
+    e = jnp.where(m == 4, n, jnp.where(m == 5, n + 14, 2 * n + m - 6))
+    upper = e >= EXTRA
+    helps = jnp.where(m == 4, n < 14, jnp.where(m == 5, n < 6, e < 2 * EXTRA))
+    owner = jnp.where(upper, 1, 0) + jnp.where(m >= 6, 2, 0)
+    own_slot = jnp.where(m == 4, n - 14, jnp.where(m == 5, n - 6, e - 12))
+    o = jnp.where(m < 4, m, jnp.where(helps, owner, jnp.where(m == 5, 5, 4)))
+    s = jnp.where(
+        m < 4, n, jnp.where(helps, OWN + e - jnp.where(upper, EXTRA, 0), own_slot)
+    )
+    unit = o * PER + s
+    return jnp.where(right, XR * PER - 1 - unit, unit)
 
 
 def x_gather(u_ref, out_ref):
     low_half = lax.broadcasted_iota(jnp.int32, (UNIT, 128), 1) < 64
-    per = XS // UNIT
-    split = SIDE % per
-    for first, last in ((0, split), (split, per)):
+    split = SIDE % PER
+    for first, last in ((0, split), (split, PER)):
         def back(i, carry):
             at = pl.multiple_of(i * UNIT, UNIT)
             for h in range(2):
@@ -377,14 +417,15 @@
                     for res in range(XR)
                 ]
                 for g, (re, im) in enumerate(small_dft(values, -1)):
-                    if g * per + first < SIDE:
-                        flat = g * per + i
-                    elif g * per + first >= SIDE + SKIP:
-                        flat = g * per + i - SKIP
+                    if g * PER + first < SIDE:
+                        m, side, u = place_of(g, i)
+                    elif (XR - g) * PER - last < SIDE:
+                        m, side, u = place_of(XR - 1 - g, PER - 1 - i)
+                        m = XR - 1 - m
                     else:
                         continue
-                    worker = flat // UNITS
-                    line = pl.ds(pl.multiple_of((flat - worker * UNITS) * UNIT, UNIT), UNIT)
+                    worker = 2 * m + side
+                    line = pl.ds(pl.multiple_of(u * UNIT, UNIT), UNIT)
                     if h == 0:
                         out_ref[worker, 0, line, :] = re
                         out_ref[worker, 1, line, :] = im
@@ -394,11 +435,7 @@
         lax.fori_loop(first, last, back, 0)
 
 
-def unit_of(flat):
-    return jnp.where(flat < SIDE, flat, flat + SKIP)
-
-
-def z_forward(first_unit, row, rows, v_ref, high_ref, low_ref, out_ref, w_ref):
+def z_forward(unit_of, row, rows, v_ref, high_ref, low_ref, out_ref, w_ref):
     low_half = lax.broadcasted_iota(jnp.int32, (rows, 128), 1) < 64
 
     def group(r, carry):
@@ -426,7 +463,7 @@
 
     def body(i, carry):
         at = pl.multiple_of(i * UNIT, UNIT)
-        along = unit_of(first_unit + i) * UNIT + lax.broadcasted_iota(jnp.int32, (UNIT, 128), 0)
+        along = unit_of(row // UNIT + i) * UNIT + lax.broadcasted_iota(jnp.int32, (UNIT, 128), 0)
         along = jnp.where(2 * along < NX, along, along - NX)
         wave_along = along.astype(jnp.float32) * (TWO_PI / NX)
         keep_along = 3 * jnp.abs(along) < NX
@@ -472,7 +509,7 @@
     count = 2 * XR
     me = 2 * gx + gz
     half = own_ref.shape[2]
-    rows = half // CHUNKS
+    offsets = [sum(CHUNKS[:c]) for c in range(len(CHUNKS))]
 
     def device(t):
         return (t // 2, lax.rem(t, 2))
@@ -493,26 +530,26 @@
 
     def load_own(c):
         return pltpu.make_async_copy(
-            velocity_ref.at[:, :, pl.ds(pl.multiple_of(gz * half + c * rows, rows), rows), :],
-            own_ref.at[:, :, pl.ds(pl.multiple_of(c * rows, rows), rows), :],
+            velocity_ref.at[:, :, pl.ds(pl.multiple_of(gz * half + offsets[c], 16), CHUNKS[c]), :],
+            own_ref.at[:, :, pl.ds(offsets[c], CHUNKS[c]), :],
             own_sems.at[c],
         )
 
     def swap(c):
         return pltpu.make_async_remote_copy(
             src_ref=velocity_ref.at[
-                :, :, pl.ds(pl.multiple_of((1 - gz) * half + c * rows, rows), rows), :
+                :, :, pl.ds(pl.multiple_of((1 - gz) * half + offsets[c], 16), CHUNKS[c]), :
             ],
-            dst_ref=other_ref.at[:, :, pl.ds(pl.multiple_of(c * rows, rows), rows), :],
+            dst_ref=other_ref.at[:, :, pl.ds(offsets[c], CHUNKS[c]), :],
             send_sem=swap_send.at[c],
             recv_sem=swap_recv.at[c],
             device_id=(gx, 1 - gz),
             device_id_type=pl.DeviceIdType.MESH,
         )
 
-    for c in range(CHUNKS):
+    for c in range(len(CHUNKS)):
         load_own(c).start()
-    for table in tables:
+    for table in tables[:2]:
         table.start()
 
     barrier = pltpu.get_barrier_semaphore()
@@ -528,8 +565,10 @@
 
     lax.fori_loop(1, count, greet, 0)
     pl.semaphore_wait(barrier, count - 1)
-    for c in range(CHUNKS):
+    for c in range(len(CHUNKS)):
         swap(c).start()
+    for table in tables[2:]:
+        table.start()
 
     def ship(src_ref, dst_ref, sends, recvs, c, at, length):
         span = pl.ds(at, length)
@@ -545,9 +584,11 @@
                 device_id_type=pl.DeviceIdType.MESH,
             )
 
-        local = pltpu.make_async_copy(
-            src_ref.at[me, :, span, :], dst_ref.at[me, :, span, :], recvs.at[c, 0]
-        )
+        def local():
+            return pltpu.make_async_copy(
+                src_ref.at[me, :, span, :], dst_ref.at[me, :, span, :], recvs.at[c, 0]
+            )
+
         return copy, local
 
     def ship_start(*args):
@@ -558,7 +599,7 @@
             return carry
 
         lax.fori_loop(1, count, start, 0)
-        local.start()
+        local().start()
 
     def ship_arrive(*args):
         copy, local = ship(*args)
@@ -568,7 +609,7 @@
             return carry
 
         lax.fori_loop(1, count, wait, 0)
-        local.wait()
+        local().wait()
 
     def ship_leave(*args):
         copy, _ = ship(*args)
@@ -580,74 +621,60 @@
         lax.fori_loop(1, count, wait, 0)
 
     def spread_args(c):
-        return out_ref, in_ref, out_send, out_recv, c, pl.multiple_of(c * rows, rows), rows
+        return out_ref, in_ref, out_send, out_recv, c, offsets[c], CHUNKS[c]
 
     tables[0].wait()
     tables[1].wait()
-
-    def inverse(c, carry):
+    for c in range(len(CHUNKS)):
         load_own(c).wait()
         swap(c).wait_recv()
         z_inverse(
-            gz == 0, own_ref, other_ref, pl.multiple_of(c * rows, rows), rows,
+            gz == 0, own_ref, other_ref, offsets[c], CHUNKS[c],
             zh_ref, zl_ref, out_ref, zth_ref, ztl_ref,
         )
         ship_start(*spread_args(c))
-        return carry
-
-    lax.fori_loop(0, CHUNKS, inverse, 0)
-
-    def spread(c, carry):
+
+    for c in range(len(CHUNKS)):
         ship_arrive(*spread_args(c))
-        x_spread(in_ref, pl.multiple_of(c * rows, rows), rows, th_ref, tl_ref)
-        return carry
-
-    lax.fori_loop(0, CHUNKS, spread, 0)
+        x_spread(in_ref, offsets[c], CHUNKS[c], th_ref, tl_ref)
     for table in tables[2:]:
         table.wait()
     x_products(ih_ref, il_ref, fh_ref, fl_ref, th_ref, tl_ref, u_ref)
     x_gather(u_ref, back_ref)
 
-    def back_args(c, units):
-        at = pl.multiple_of(c * LARGE * UNIT, UNIT)
-        return back_ref, work_ref, back_send, back_recv, c, at, units * UNIT
-
-    last = UNITS - LARGE * (SPANS - 1)
-
-    def over_spans(step):
-        def one(c, carry):
-            step(c, LARGE)
-            return carry
-
-        lax.fori_loop(0, SPANS - 1, one, 0)
-        step(SPANS - 1, last)
-
-    over_spans(lambda c, units: ship_start(*back_args(c, units)))
-
-    per = XS // UNIT
+    starts = [sum(SPANS[:c]) for c in range(len(SPANS))]
+
+    def back_args(c):
+        return back_ref, work_ref, back_send, back_recv, c, starts[c] * UNIT, SPANS[c] * UNIT
+
+    for c in range(BACK_AHEAD):
+        ship_start(*back_args(c))
 
     def result(u, side):
-        unit = unit_of(UNITS * me + u)
-        owner = unit // per
-        slot = unit - owner * per
+        unit = unit_at(gx, gz, u)
+        owner = unit // PER
+        slot = unit - owner * PER
         src = res_ref.at[side, :, pl.ds(pl.multiple_of(u * UNIT, UNIT), UNIT), :]
         dst = term_ref.at[:, pl.ds(pl.multiple_of(slot * UNIT, UNIT), UNIT), :]
         here = jnp.logical_and(owner == gx, side == gz)
-        remote = pltpu.make_async_remote_copy(
-            src_ref=src,
-            dst_ref=dst,
-            send_sem=res_send.at[side, u],
-            recv_sem=res_recv.at[slot],
-            device_id=(owner, side),
-            device_id_type=pl.DeviceIdType.MESH,
-        )
-        return here, remote, pltpu.make_async_copy(src, dst, res_recv.at[slot])
-
-    def forward(c, units):
-        ship_arrive(*back_args(c, units))
-        unit = c * LARGE
+
+        def remote():
+            return pltpu.make_async_remote_copy(
+                src_ref=src,
+                dst_ref=dst,
+                send_sem=res_send.at[side, u],
+                recv_sem=res_recv.at[slot],
+                device_id=(owner, side),
+                device_id_type=pl.DeviceIdType.MESH,
+            )
+
+        return here, remote, lambda: pltpu.make_async_copy(src, dst, res_recv.at[slot])
+
+    for c in range(len(SPANS)):
+        ship_arrive(*back_args(c))
+        unit, units = starts[c], SPANS[c]
         z_forward(
-            UNITS * me + unit, pl.multiple_of(unit * UNIT, UNIT), units * UNIT,
+            functools.partial(unit_at, gx, gz), unit * UNIT, units * UNIT,
             work_ref, zh_ref, zl_ref, res_ref, w_ref,
         )
 
@@ -657,16 +684,16 @@
 
                 @pl.when(here)
                 def _():
-                    local.start()
+                    local().start()
 
                 @pl.when(jnp.logical_not(here))
                 def _():
-                    remote.start()
+                    remote().start()
             return carry
 
         lax.fori_loop(0, units, send, 0)
-
-    over_spans(forward)
+        if c + BACK_AHEAD < len(SPANS):
+            ship_start(*back_args(c + BACK_AHEAD))
 
     def sent(u, carry):
         for side in range(2):
@@ -674,13 +701,13 @@
 
             @pl.when(jnp.logical_not(here))
             def _():
-                remote.wait_send()
+                remote().wait_send()
         return carry
 
     def got(s, carry):
-        unit = gx * per + s
-
-        @pl.when(jnp.logical_or(unit < SIDE, unit >= SIDE + SKIP))
+        unit = gx * PER + s
+
+        @pl.when(jnp.logical_or(unit < SIDE, unit >= XR * PER - SIDE))
         def _():
             pltpu.make_async_copy(
                 res_ref.at[0, :, pl.ds(0, UNIT), :],
@@ -689,23 +716,21 @@
             ).wait()
         return carry
 
-    lax.fori_loop(0, per, got, 0)
+    lax.fori_loop(0, PER, got, 0)
     lax.fori_loop(0, UNITS, sent, 0)
 
-    def swap_left(c, carry):
+    for c in range(len(CHUNKS)):
         swap(c).wait_send()
         ship_leave(*spread_args(c))
-        return carry
-
-    lax.fori_loop(0, CHUNKS, swap_left, 0)
-    over_spans(lambda c, units: ship_leave(*back_args(c, units)))
+    for c in range(len(SPANS)):
+        ship_leave(*back_args(c))
 
 
 def advance_kernel(place_ref, base_ref, v_ref, old_ref, term_ref, along_ref, across_ref, next_ref, non_ref):
     rows, extent = v_ref.shape[2:]
-    unit = place_ref[0] * (XS // UNIT) + pl.program_id(0) * (rows // UNIT)
+    unit = place_ref[0] * PER + pl.program_id(0) * (rows // UNIT)
     lower = place_ref[1] == 0
-    active = jnp.logical_or(unit < SIDE, unit >= SIDE + SKIP)
+    active = jnp.logical_or(unit < SIDE, unit >= XR * PER - SIDE)
     wave_along = along_ref[:, :1]
     wave_across = across_ref[:1, :]
     damping = jnp.exp(-VISCOSITY * (wave_along * wave_along + wave_across * wave_across))
@@ -731,7 +756,7 @@
     velocity, previous = velocity[:, :, 0], previous[:, :, 0]
     mode_count, extent = velocity.shape[2:]
     half = mode_count // 2
-    rows = half // CHUNKS
+    rows = max(CHUNKS)
     gx, gz = lax.axis_index("gx"), lax.axis_index("gz")
     f32, bf16 = jnp.float32, jnp.bfloat16
     zh, zl = z_table()
@@ -764,18 +789,18 @@
             pltpu.VMEM((XR, 2 * XS, 256), f32),
             pltpu.VMEM((count, 3, UNITS * UNIT, 128), f32),
             pltpu.VMEM((count, 3, UNITS * UNIT, 128), f32),
-            pltpu.VMEM((ZR, 3 * LARGE * UNIT, 2 * ZS), f32),
+            pltpu.VMEM((ZR, 3 * max(SPANS) * UNIT, 2 * ZS), f32),
             pltpu.VMEM((2, 4, UNITS * UNIT, active), f32),
             dma((6,)),
-            dma((CHUNKS,)),
-            dma((CHUNKS,)),
-            dma((CHUNKS,)),
-            dma((CHUNKS, count)),
-            dma((CHUNKS, count)),
-            dma((SPANS, count)),
-            dma((SPANS, count)),
+            dma((len(CHUNKS),)),
+            dma((len(CHUNKS),)),
+            dma((len(CHUNKS),)),
+            dma((len(CHUNKS), count)),
+            dma((len(CHUNKS), count)),
+            dma((len(SPANS), count)),
+            dma((len(SPANS), count)),
             dma((2, UNITS)),
-            dma((XS // UNIT,)),
+            dma((PER,)),
         ],
         compiler_params=pltpu.CompilerParams(
             collective_id=1, has_side_effects=True, vmem_limit_bytes=60 * MIB
@@ -809,7 +834,7 @@
             pl.BlockSpec((8, extent), lambda i: (0, 0)),
         ],
         out_specs=[field, field],
-        compiler_params=pltpu.CompilerParams(vmem_limit_bytes=48 * MIB),
+        compiler_params=pltpu.CompilerParams(vmem_limit_bytes=60 * MIB),
         name="advance",
     )(
         jnp.stack([gx, gz]).astype(jnp.int32),

time: 266 us -> 252 us (0.947)
  Pallas kernels: 262 us -> 249 us
    pallas_call x1, Pallas kernels: 254 us -> 240 us  [lines_local(): pl.pallas_call(substep_kernel, out_shape=jax.ShapeDtypeStruct((4, mode_co...]
where the time goes in v2:
time: 252 us
  Pallas kernels  249 us (99%)
    pallas_call x1, Pallas kernels, lines_local(): pl.pallas_call(substep_kernel, out_shape=jax.ShapeDtypeStruct((4, mode_co...  240 us
    pallas_call x1, Pallas kernels, lines_local(): pl.pallas_call(advance_kernel, grid=(mode_count // block,), out_shape=[ja...  8.71 us

profile of v2, /device:TPU:12, one launch (start us, length us, event | category | flops | bytes accessed | tf_op | source)
XLA Modules:
  0.0 252.3 jit_solution(16135433179115582283)
XLA Ops:
  1.3 0.6 pad_add_fusion.place_ref
  1.9 0.6 broadcast_in_dim.9.across_ref
  2.5 0.7 broadcast_in_dim.8.along_ref
  3.2 240.3 %substep.1.term_ref = f32[4,256,768]{2,1,0:T(8,128)} custom-call(f32[2,2,256,1024]{3,2,1,0:T(8,128)} %bitcast.10, bf16[8,256,512]{2,1,0:T(8,128)(2,1)} %constant.39.clone.zh_hbm, bf16[8,256,512]{2,1,0:T(8,128)(2,1)} %constant.40.clone.zl_hbm, bf16[16,256,512]{2,1,0:T(8,128)(2,1)} %constant.41.clone.ih_hbm, bf16[16,256,512]{2,1,0:T(8,128)(2,1)} %constant.42.clone.il_hbm, ...), custom_call_target="tpu_custom_call" | custom-call | flops 10000000000 | bytes 67108864 | tf_op jit(solution)/shard_map/substep/pallas_call | solution.py:769
  243.6 8.7 %advance.1 = (f32[2,2,256,1024]{3,2,1,0:T(8,128)}, f32[2,2,256,1024]{3,2,1,0:T(8,128)}) custom-call(s32[2]{0:T(128)} %pad_add_fusion.place_ref, f32[1]{0:T(128)S(6)} %copy.13.base_ref, f32[2,2,256,1024]{3,2,1,0:T(8,128)} %bitcast.11, f32[2,2,256,1024]{3,2,1,0:T(8,128)} %bitcast.12, f32[4,256,768]{2,1,0:T(8,128)} %substep.1.term_ref, ...), custom_call_target="tpu_custom_call" | custom-call | tf_op jit(solution)/shard_map/advance/pallas_call | solution.py:823
  (2 shorter events, 0.0 us)

commit v3 on v2

--- a/solution.py
+++ b/solution.py
@@ -208,16 +208,24 @@
 LOW = (0, 1, 2)
 HIGH = (5, 6, 7)
 MIB = 1 << 20
-CHUNKS = (16, 16, 32, 32, 32)
+CHUNKS = (16,) * 8
 UNIT = 8
 UNITS = 11
 SIDE = 16 * UNITS
 PER = XS // UNIT
 OWN = 2 * UNITS
 EXTRA = PER - OWN
-SPANS = (2, 2, 2, 2, 2, 1)
-BACK_AHEAD = 6
+SPANS = (3, 3, 3, 1, 1)
+BACK_AHEAD = 3
 UNROLL = 16
+UNROLL_INV = 8
+UNROLL_FWD = 8
+UNROLL_EARLY = 4
+BLOCK = 32
+SUB_VMEM = 49
+ADV_VMEM = 40
+SHORT = 9
+NEEDED = SIDE - 4
 
 
 def split_table(table):
@@ -241,7 +249,20 @@
     m = np.arange(XS)[None, None, :]
     angle = TWO_PI / NX * ((m * (r + XR * s)) % NX)
     cos, sin = np.cos(angle) / math.sqrt(NX), np.sin(angle) / math.sqrt(NX)
-    return split_table(np.concatenate([cos, -sin], axis=2))
+    return np.stack([cos, -sin], axis=2)
+
+
+def x_inverse_table():
+    table = x_table().reshape(XR, XS, 4, XS // 2)
+    parts = []
+    for c, length in enumerate(CHUNKS):
+        start = sum(CHUNKS[:c])
+        parts.append(table[..., start : start + length].reshape(XR, XS, 4 * length))
+    return split_table(np.concatenate(parts, axis=2))
+
+
+def x_forward_table():
+    return split_table(np.swapaxes(x_table().reshape(XR, XS, 2 * XS), 1, 2))
 
 
 def turn(value, numerator, size, sign):
@@ -296,7 +317,7 @@
     )
 
 
-def z_inverse(first, own_ref, other_ref, row, rows, high_ref, low_ref, out_ref, th_ref, tl_ref):
+def z_inverse(first, rows_ref, row, rows, high_ref, low_ref, out_ref, th_ref, tl_ref):
     step = 16
     for c in range(2):
         def body(i, carry):
@@ -305,8 +326,8 @@
                 values = [None] * ZR
                 for a in range(ZR // 2):
                     to = (pl.ds(row + at, step), pl.ds(a * ZS + lane, 128))
-                    own = [own_ref[(c, p) + to] for p in range(2)]
-                    other = [other_ref[(c, p) + to] for p in range(2)]
+                    own = [rows_ref[(0, 2 * c + p) + to] for p in range(2)]
+                    other = [rows_ref[(1, 2 * c + p) + to] for p in range(2)]
                     values[a] = tuple(jnp.where(first, x, y) for x, y in zip(own, other))
                     values[a + ZR // 2] = tuple(jnp.where(first, y, x) for x, y in zip(own, other))
                 for r, pair in enumerate(small_dft(values, 1)):
@@ -334,34 +355,54 @@
                 out_ref[r * 4 + 2 * t, p, pl.ds(row, rows), :] = even
                 out_ref[r * 4 + 2 * t + 1, p, pl.ds(row, rows), :] = odd
         return carry
-    lax.fori_loop(0, ZR, group, 0)
+    lax.fori_loop(0, ZR, group, 0, unroll=UNROLL_INV)
 
 
 def x_spread(v_ref, row, rows, th_ref, tl_ref):
     step = 16
-    half = XS // 2
     for r in range(2):
         def body(i, carry):
-            at = pl.multiple_of(row + i * step, step)
+            at = pl.multiple_of(i * step, step)
             values = [
-                tuple(v_ref[2 * g + r, p, pl.ds(at, step), :] for p in range(2)) for g in range(XR)
+                tuple(v_ref[2 * g + r, p, pl.ds(row + at, step), :] for p in range(2))
+                for g in range(XR)
             ]
             for res, pair in enumerate(small_dft(values, 1)):
                 for p in range(2):
                     high, low = parts_of(pair[p])
-                    th_ref[res, pl.ds(p * XS + r * half + at, step), :] = high
-                    tl_ref[res, pl.ds(p * XS + r * half + at, step), :] = low
+                    line = pl.ds(4 * row + (2 * p + r) * rows + at, step)
+                    th_ref[res, line, :] = high
+                    tl_ref[res, line, :] = low
             return carry
         lax.fori_loop(0, rows // step, body, 0)
 
 
-def x_products(ih_ref, il_ref, fh_ref, fl_ref, th_ref, tl_ref, u_ref):
+def x_early(lines, ih_ref, il_ref, th_ref, tl_ref, f_ref):
     def residue(res, carry):
-        field = dot3(ih_ref[res], il_ref[res], th_ref[res], tl_ref[res], ((1,), (0,)))
+        f_ref[res] = dot3(
+            ih_ref[res, :, :lines], il_ref[res, :, :lines],
+            th_ref[res, :lines], tl_ref[res, :lines], ((1,), (0,)),
+        )
+        return carry
+    lax.fori_loop(0, XR, residue, 0, unroll=UNROLL_EARLY)
+
+
+def x_products(lines, ih_ref, il_ref, fh_ref, fl_ref, th_ref, tl_ref, f_ref, u_refs):
+    def residue(res, carry):
+        field = f_ref[res] + dot3(
+            ih_ref[res, :, lines:], il_ref[res, :, lines:],
+            th_ref[res, lines:], tl_ref[res, lines:], ((1,), (0,)),
+        )
         swapped = pltpu.roll(field, 64, 1)
         products = jnp.concatenate([field * field, field * swapped], axis=1)
         high, low = parts_of(products)
-        u_ref[res] = dot3(fh_ref[res], fl_ref[res], high, low, ((1,), (0,)))
+        both = dot3(fh_ref[res], fl_ref[res], high, low, ((1,), (0,)))
+        half = XS // 2
+        for h, u_ref in enumerate(u_refs):
+            for p in range(2):
+                for r in range(2):
+                    at = p * XS + r * half
+                    u_ref[2 * res + p, r] = both[at : at + half, h * 128 : h * 128 + 128]
         return carry
     lax.fori_loop(0, XR, residue, 0, unroll=UNROLL)
 
@@ -402,16 +443,17 @@
     return jnp.where(right, XR * PER - 1 - unit, unit)
 
 
-def x_gather(u_ref, out_ref):
+def x_gather(u_refs, out_ref):
     low_half = lax.broadcasted_iota(jnp.int32, (UNIT, 128), 1) < 64
     split = SIDE % PER
     for first, last in ((0, split), (split, PER)):
         def back(i, carry):
-            at = pl.multiple_of(i * UNIT, UNIT)
+            part = i * UNIT // (XS // 2)
+            at = pl.multiple_of(i * UNIT - part * (XS // 2), UNIT)
             for h in range(2):
                 values = [
                     tuple(
-                        u_ref[res, pl.ds(p * XS + at, UNIT), pl.ds(h * 128, 128)]
+                        u_refs[h][2 * res + p, part, pl.ds(at, UNIT), :]
                         for p in range(2)
                     )
                     for res in range(XR)
@@ -459,7 +501,7 @@
         w_ref[r, : 3 * rows, :ZS] = cos[: 3 * rows] + sin[3 * rows :]
         w_ref[r, : 3 * rows, ZS:] = cos[3 * rows :] - sin[: 3 * rows]
         return carry
-    lax.fori_loop(0, ZR, group, 0)
+    lax.fori_loop(0, ZR, group, 0, unroll=UNROLL_FWD)
 
     def body(i, carry):
         at = pl.multiple_of(i * UNIT, UNIT)
@@ -498,17 +540,17 @@
 
 
 def substep_kernel(
-    velocity_ref, zh_hbm, zl_hbm, ih_hbm, il_hbm, fh_hbm, fl_hbm,
+    velocity_ref, tables_hbm, fh_hbm, fl_hbm,
     term_ref,
-    own_ref, other_ref, zh_ref, zl_ref, ih_ref, il_ref, fh_ref, fl_ref,
-    zth_ref, ztl_ref, out_ref, in_ref, th_ref, tl_ref, u_ref, back_ref, work_ref, w_ref, res_ref,
+    rows_ref, zh_ref, zl_ref, ih_ref, il_ref, fh_ref, fl_ref,
+    zth_ref, ztl_ref, out_ref, in_ref, th_ref, tl_ref, f_ref, back_ref, work_ref, w_ref,
     table_sems, own_sems, swap_send, swap_recv, out_send, out_recv, back_send, back_recv,
     res_send, res_recv,
 ):
     gx, gz = lax.axis_index("gx"), lax.axis_index("gz")
     count = 2 * XR
     me = 2 * gx + gz
-    half = own_ref.shape[2]
+    half = rows_ref.shape[2]
     offsets = [sum(CHUNKS[:c]) for c in range(len(CHUNKS))]
 
     def device(t):
@@ -518,10 +560,10 @@
         pltpu.make_async_copy(src, dst, table_sems.at[n])
         for n, (src, dst) in enumerate(
             (
-                (zh_hbm, zh_ref),
-                (zl_hbm, zl_ref),
-                (ih_hbm, ih_ref),
-                (il_hbm, il_ref),
+                (tables_hbm.at[pl.ds(0, ZR)], zh_ref),
+                (tables_hbm.at[pl.ds(ZR, ZR)], zl_ref),
+                (tables_hbm.at[pl.ds(2 * ZR, XR)], ih_ref),
+                (tables_hbm.at[pl.ds(2 * ZR + XR, XR)], il_ref),
                 (fh_hbm, fh_ref),
                 (fl_hbm, fl_ref),
             )
@@ -530,17 +572,17 @@
 
     def load_own(c):
         return pltpu.make_async_copy(
-            velocity_ref.at[:, :, pl.ds(pl.multiple_of(gz * half + offsets[c], 16), CHUNKS[c]), :],
-            own_ref.at[:, :, pl.ds(offsets[c], CHUNKS[c]), :],
+            velocity_ref.at[:, pl.ds(pl.multiple_of(gz * half + offsets[c], 16), CHUNKS[c]), :],
+            rows_ref.at[0, :, pl.ds(offsets[c], CHUNKS[c]), :],
             own_sems.at[c],
         )
 
     def swap(c):
         return pltpu.make_async_remote_copy(
             src_ref=velocity_ref.at[
-                :, :, pl.ds(pl.multiple_of((1 - gz) * half + offsets[c], 16), CHUNKS[c]), :
+                :, pl.ds(pl.multiple_of((1 - gz) * half + offsets[c], 16), CHUNKS[c]), :
             ],
-            dst_ref=other_ref.at[:, :, pl.ds(offsets[c], CHUNKS[c]), :],
+            dst_ref=rows_ref.at[1, :, pl.ds(offsets[c], CHUNKS[c]), :],
             send_sem=swap_send.at[c],
             recv_sem=swap_recv.at[c],
             device_id=(gx, 1 - gz),
@@ -591,15 +633,26 @@
 
         return copy, local
 
+    def takes(t, src_ref, dst_ref, sends, recvs, c, at, length):
+        if dst_ref is not work_ref or at < SHORT * UNIT:
+            return t >= 0
+        g = t // 2
+        return jnp.logical_and(g != 5, g != XR - 6)
+
     def ship_start(*args):
         copy, local = ship(*args)
 
         def start(i, carry):
-            copy(i).start()
+            @pl.when(takes(lax.rem(me + i, count), *args))
+            def _():
+                copy(i).start()
             return carry
 
         lax.fori_loop(1, count, start, 0)
-        local().start()
+
+        @pl.when(takes(me, *args))
+        def _():
+            local().start()
 
     def ship_arrive(*args):
         copy, local = ship(*args)
@@ -615,7 +668,9 @@
         copy, _ = ship(*args)
 
         def wait(i, carry):
-            copy(i).wait_send()
+            @pl.when(takes(lax.rem(me + i, count), *args))
+            def _():
+                copy(i).wait_send()
             return carry
 
         lax.fori_loop(1, count, wait, 0)
@@ -629,7 +684,7 @@
         load_own(c).wait()
         swap(c).wait_recv()
         z_inverse(
-            gz == 0, own_ref, other_ref, offsets[c], CHUNKS[c],
+            gz == 0, rows_ref, offsets[c], CHUNKS[c],
             zh_ref, zl_ref, out_ref, zth_ref, ztl_ref,
         )
         ship_start(*spread_args(c))
@@ -637,10 +692,16 @@
     for c in range(len(CHUNKS)):
         ship_arrive(*spread_args(c))
         x_spread(in_ref, offsets[c], CHUNKS[c], th_ref, tl_ref)
-    for table in tables[2:]:
-        table.wait()
-    x_products(ih_ref, il_ref, fh_ref, fl_ref, th_ref, tl_ref, u_ref)
-    x_gather(u_ref, back_ref)
+        if c == len(CHUNKS) - 2:
+            for table in tables[2:]:
+                table.wait()
+            x_early(4 * offsets[-1], ih_ref, il_ref, th_ref, tl_ref, f_ref)
+    for c in range(len(CHUNKS)):
+        ship_leave(*spread_args(c))
+    x_products(
+        4 * offsets[-1], ih_ref, il_ref, fh_ref, fl_ref, th_ref, tl_ref, f_ref, (out_ref, in_ref)
+    )
+    x_gather((out_ref, in_ref), back_ref)
 
     starts = [sum(SPANS[:c]) for c in range(len(SPANS))]
 
@@ -654,7 +715,9 @@
         unit = unit_at(gx, gz, u)
         owner = unit // PER
         slot = unit - owner * PER
-        src = res_ref.at[side, :, pl.ds(pl.multiple_of(u * UNIT, UNIT), UNIT), :]
+        src = rows_ref.at[
+            side, :, pl.ds(pl.multiple_of(u * UNIT, UNIT), UNIT), pl.ds(0, term_ref.shape[2])
+        ]
         dst = term_ref.at[:, pl.ds(pl.multiple_of(slot * UNIT, UNIT), UNIT), :]
         here = jnp.logical_and(owner == gx, side == gz)
 
@@ -670,12 +733,12 @@
 
         return here, remote, lambda: pltpu.make_async_copy(src, dst, res_recv.at[slot])
 
-    for c in range(len(SPANS)):
+    def forward(c):
         ship_arrive(*back_args(c))
         unit, units = starts[c], SPANS[c]
         z_forward(
             functools.partial(unit_at, gx, gz), unit * UNIT, units * UNIT,
-            work_ref, zh_ref, zl_ref, res_ref, w_ref,
+            work_ref, zh_ref, zl_ref, rows_ref, w_ref,
         )
 
         def send(n, carry):
@@ -692,6 +755,12 @@
             return carry
 
         lax.fori_loop(0, units, send, 0)
+
+    for c in range(len(SPANS)):
+        @pl.when(takes(me, *back_args(c)))
+        def _():
+            forward(c)
+
         if c + BACK_AHEAD < len(SPANS):
             ship_start(*back_args(c + BACK_AHEAD))
 
@@ -707,49 +776,87 @@
     def got(s, carry):
         unit = gx * PER + s
 
-        @pl.when(jnp.logical_or(unit < SIDE, unit >= XR * PER - SIDE))
+        @pl.when(jnp.logical_or(unit < NEEDED, unit >= XR * PER - NEEDED))
         def _():
             pltpu.make_async_copy(
-                res_ref.at[0, :, pl.ds(0, UNIT), :],
+                rows_ref.at[0, :, pl.ds(0, UNIT), pl.ds(0, term_ref.shape[2])],
                 term_ref.at[:, pl.ds(pl.multiple_of(s * UNIT, UNIT), UNIT), :],
                 res_recv.at[s],
             ).wait()
         return carry
 
     lax.fori_loop(0, PER, got, 0)
-    lax.fori_loop(0, UNITS, sent, 0)
+    short = jnp.logical_or(gx == 5, gx == XR - 6)
+    lax.fori_loop(0, jnp.where(short, SHORT, UNITS), sent, 0)
 
     for c in range(len(CHUNKS)):
         swap(c).wait_send()
-        ship_leave(*spread_args(c))
     for c in range(len(SPANS)):
         ship_leave(*back_args(c))
 
 
-def advance_kernel(place_ref, base_ref, v_ref, old_ref, term_ref, along_ref, across_ref, next_ref, non_ref):
-    rows, extent = v_ref.shape[2:]
-    unit = place_ref[0] * PER + pl.program_id(0) * (rows // UNIT)
-    lower = place_ref[1] == 0
-    active = jnp.logical_or(unit < SIDE, unit >= XR * PER - SIDE)
-    wave_along = along_ref[:, :1]
-    wave_across = across_ref[:1, :]
-    damping = jnp.exp(-VISCOSITY * (wave_along * wave_along + wave_across * wave_across))
-    shear = base_ref[0] * wave_along
-    empty = jnp.zeros((rows, extent - term_ref.shape[2]), jnp.float32)
-    for c in range(2):
-        for p in range(2):
-            term = jnp.where(active, term_ref[2 * c + p], 0.0)
-            term = jnp.where(
-                lower,
-                jnp.concatenate([term, empty], axis=1),
-                jnp.concatenate([empty, term], axis=1),
-            )
-            other = shear * v_ref[c, 1 - p]
-            result = term + other if p == 0 else term - other
-            non_ref[c, p] = result
-            next_ref[c, p] = damping * (
-                v_ref[c, p] + TIME_STEP * (GAMMA_NEW * result + ZETA_OLD * old_ref[c, p])
-            )
+def advance_kernel(
+    base_ref, v_ref, old_ref, term_ref, next_hbm, non_hbm, next_ref, non_ref, store_sems
+):
+    mode_count, extent = v_ref.shape[2:]
+    lower = lax.axis_index("gz") == 0
+    across = lax.axis_index("gz") * extent + lax.broadcasted_iota(jnp.int32, (1, extent), 1)
+    wave_across = jnp.where(2 * across < NZ, across, across - NZ).astype(jnp.float32) * (TWO_PI / NZ)
+    empty = jnp.zeros((UNIT, extent - term_ref.shape[2]), jnp.float32)
+
+    def at(c):
+        return pl.ds(pl.multiple_of(c * BLOCK, BLOCK), BLOCK)
+
+    def stores(c):
+        return (
+            pltpu.make_async_copy(
+                next_ref.at[:, :, at(c), :], next_hbm.at[:, :, at(c), :], store_sems.at[0, c]
+            ),
+            pltpu.make_async_copy(
+                non_ref.at[:, :, at(c), :], non_hbm.at[:, :, at(c), :], store_sems.at[1, c]
+            ),
+        )
+
+    def work(c, carry):
+        def lines(i, carry):
+            row = pl.multiple_of(c * BLOCK + i * UNIT, UNIT)
+            start = lax.axis_index("gx") * XS + row
+            active = jnp.logical_or(start < NEEDED * UNIT, start >= NX - NEEDED * UNIT)
+            along = start + lax.broadcasted_iota(jnp.int32, (UNIT, 1), 0)
+            wave_along = jnp.where(2 * along < NX, along, along - NX).astype(jnp.float32) * (TWO_PI / NX)
+            damping = jnp.exp(-VISCOSITY * (wave_along * wave_along + wave_across * wave_across))
+            shear = base_ref[0] * wave_along
+            to = pl.ds(row, UNIT)
+            for f in range(2):
+                for p in range(2):
+                    term = jnp.where(active, term_ref[2 * f + p, to, :], 0.0)
+                    term = jnp.where(
+                        lower,
+                        jnp.concatenate([term, empty], axis=1),
+                        jnp.concatenate([empty, term], axis=1),
+                    )
+                    other = shear * v_ref[f, 1 - p, to, :]
+                    result = term + other if p == 0 else term - other
+                    non_ref[f, p, to, :] = result
+                    next_ref[f, p, to, :] = damping * (
+                        v_ref[f, p, to, :]
+                        + TIME_STEP * (GAMMA_NEW * result + ZETA_OLD * old_ref[f, p, to, :])
+                    )
+            return carry
+
+        lax.fori_loop(0, BLOCK // UNIT, lines, 0)
+        for store in stores(c):
+            store.start()
+        return carry
+
+    lax.fori_loop(0, mode_count // BLOCK, work, 0)
+
+    def end(c, carry):
+        for store in stores(c):
+            store.wait()
+        return carry
+
+    lax.fori_loop(0, mode_count // BLOCK, end, 0)
 
 
 def lines_local(velocity, previous, base_flow):
@@ -757,11 +864,10 @@
     mode_count, extent = velocity.shape[2:]
     half = mode_count // 2
     rows = max(CHUNKS)
-    gx, gz = lax.axis_index("gx"), lax.axis_index("gz")
     f32, bf16 = jnp.float32, jnp.bfloat16
     zh, zl = z_table()
-    xh, xl = x_table()
-    fh, fl = np.swapaxes(xh, 1, 2), np.swapaxes(xl, 1, 2)
+    xh, xl = x_inverse_table()
+    fh, fl = x_forward_table()
     active = len(LOW) * ZS
     count = 2 * XR
     dma = pltpu.SemaphoreType.DMA
@@ -769,11 +875,10 @@
     term = pl.pallas_call(
         substep_kernel,
         out_shape=jax.ShapeDtypeStruct((4, mode_count, active), f32),
-        in_specs=[pl.BlockSpec(memory_space=pl.ANY)] * 7,
+        in_specs=[pl.BlockSpec(memory_space=pl.ANY)] * 4,
         out_specs=pl.BlockSpec(memory_space=pl.ANY),
         scratch_shapes=[
-            pltpu.VMEM((2, 2, half, extent), f32),
-            pltpu.VMEM((2, 2, half, extent), f32),
+            pltpu.VMEM((2, 4, half, extent), f32),
             pltpu.VMEM(zh.shape, bf16),
             pltpu.VMEM(zl.shape, bf16),
             pltpu.VMEM(xh.shape, bf16),
@@ -786,11 +891,10 @@
             pltpu.VMEM((count, 2, half, 128), f32),
             pltpu.VMEM((XR, 2 * XS, 128), bf16),
             pltpu.VMEM((XR, 2 * XS, 128), bf16),
-            pltpu.VMEM((XR, 2 * XS, 256), f32),
+            pltpu.VMEM((XR, XS, 128), f32),
             pltpu.VMEM((count, 3, UNITS * UNIT, 128), f32),
             pltpu.VMEM((count, 3, UNITS * UNIT, 128), f32),
             pltpu.VMEM((ZR, 3 * max(SPANS) * UNIT, 2 * ZS), f32),
-            pltpu.VMEM((2, 4, UNITS * UNIT, active), f32),
             dma((6,)),
             dma((len(CHUNKS),)),
             dma((len(CHUNKS),)),
@@ -803,47 +907,33 @@
             dma((PER,)),
         ],
         compiler_params=pltpu.CompilerParams(
-            collective_id=1, has_side_effects=True, vmem_limit_bytes=60 * MIB
+            collective_id=1, has_side_effects=True, vmem_limit_bytes=int(SUB_VMEM * MIB)
         ),
         cost_estimate=pl.CostEstimate(
             flops=10**10, bytes_accessed=64 * velocity.size, transcendentals=0
         ),
         name="substep",
-    )(velocity, zh, zl, xh, xl, fh, fl)
-
-    def modes(start, count, size):
-        numbers = start + jnp.arange(count, dtype=jnp.int32)
-        return jnp.where(2 * numbers < size, numbers, numbers - size)
-
-    along = modes(gx * mode_count, mode_count, NX).astype(f32) * (TWO_PI / NX)
-    across = modes(gz * extent, extent, NZ).astype(f32) * (TWO_PI / NZ)
-    scalar = pl.BlockSpec(memory_space=pltpu.SMEM)
-    block = 64
-    field = pl.BlockSpec((2, 2, block, extent), lambda i: (0, 0, i, 0))
+    )(velocity.reshape(4, mode_count, extent), np.concatenate([zh, zl, xh, xl]), fh, fl)
+
+    field = pltpu.VMEM(velocity.shape, f32)
+    blocks = mode_count // BLOCK
     advanced, nonlinear = pl.pallas_call(
         advance_kernel,
-        grid=(mode_count // block,),
         out_shape=[jax.ShapeDtypeStruct(velocity.shape, f32)] * 2,
-        in_specs=[
-            scalar,
-            scalar,
+        in_specs=[pl.BlockSpec(memory_space=pltpu.SMEM)] + [pl.BlockSpec(memory_space=pltpu.VMEM)] * 3,
+        out_specs=[pl.BlockSpec(memory_space=pl.ANY)] * 2,
+        scratch_shapes=[
             field,
             field,
-            pl.BlockSpec((4, block, active), lambda i: (0, i, 0)),
-            pl.BlockSpec((block, 128), lambda i: (i, 0)),
-            pl.BlockSpec((8, extent), lambda i: (0, 0)),
+            dma((2, blocks)),
         ],
-        out_specs=[field, field],
-        compiler_params=pltpu.CompilerParams(vmem_limit_bytes=60 * MIB),
+        compiler_params=pltpu.CompilerParams(vmem_limit_bytes=ADV_VMEM * MIB),
         name="advance",
     )(
-        jnp.stack([gx, gz]).astype(jnp.int32),
         base_flow,
         velocity,
         previous,
         term,
-        jnp.broadcast_to(along[:, None], (mode_count, 128)),
-        jnp.broadcast_to(across[None], (8, extent)),
     )
     return advanced[:, :, None], nonlinear[:, :, None]
 

time: 252 us -> 246 us (0.976)
  Pallas kernels: 249 us -> 245 us
    pallas_call x1, Pallas kernels: 8.71 us -> 3.66 us  [lines_local(): pl.pallas_call(advance_kernel, out_shape=[jax.ShapeDtypeStruct(velocity.s...]
where the time goes in v3:
time: 246 us
  Pallas kernels  245 us (100%)
    pallas_call x1, Pallas kernels, lines_local(): pl.pallas_call(substep_kernel, out_shape=jax.ShapeDtypeStruct((4, mode_co...  241 us

profile of v3, /device:TPU:12, one launch (start us, length us, event | category | flops | bytes accessed | tf_op | source)
XLA Modules:
  0.0 246.3 jit_solution(17095142742503551474)
XLA Ops:
  1.3 0.0 copy-start
  1.3 0.0 copy-start.1
  1.3 241.1 %substep.1.term_ref = f32[4,256,768]{2,1,0:T(8,128)S(1)} custom-call(f32[4,256,1024]{2,1,0:T(8,128)} %bitcast.9, bf16[48,256,512]{2,1,0:T(8,128)(2,1)} %constant.6.clone.tables_hbm, bf16[16,512,256]{2,1,0:T(8,128)(2,1)} %constant.7.clone.fh_hbm, bf16[16,512,256]{2,1,0:T(8,128)(2,1)} %constant.8.clone.fl_hbm), custom_call_target="tpu_custom_call" | custom-call | flops 10000000000 | bytes 67108864 | tf_op jit(solution)/shard_map/substep/pallas_call | solution.py:875
  242.4 0.0 copy-done
  242.5 0.0 copy-done.1
  242.5 3.7 %advance.1 = (f32[2,2,256,1024]{3,2,1,0:T(8,128)}, f32[2,2,256,1024]{3,2,1,0:T(8,128)}) custom-call(f32[1]{0:T(128)S(6)} %copy.10.base_ref, f32[2,2,256,1024]{3,2,1,0:T(8,128)S(1)} %bitcast.10, f32[2,2,256,1024]{3,2,1,0:T(8,128)S(1)} %bitcast.11, f32[4,256,768]{2,1,0:T(8,128)S(1)} %substep.1.term_ref), custom_call_target="tpu_custom_call" | custom-call | tf_op jit(solution)/shard_map/advance/pallas_call | solution.py:920
Async XLA Ops:
  1.3 241.2 %copy-start = (f32[2,2,1,256,1024]{4,3,2,1,0:T(8,128)S(1)}, f32[2,2,1,256,1024]{4,3,2,1,0:T(8,128)}, u32[]{:S(2)}) copy-start(f32[2,2,1,256,1024]{4,3,2,1,0:T(8,128)} %param.6) | copy-start | bytes 12582916
  1.3 241.2 %copy-start.1 = (f32[2,2,1,256,1024]{4,3,2,1,0:T(8,128)S(1)}, f32[2,2,1,256,1024]{4,3,2,1,0:T(8,128)}, u32[]{:S(2)}) copy-start(f32[2,2,1,256,1024]{4,3,2,1,0:T(8,128)} %param.7) | copy-start | bytes 12582916

commit v4 on v3

--- a/solution.py
+++ b/solution.py
@@ -612,23 +612,26 @@
     for table in tables[2:]:
         table.start()
 
+    def target(i, c):
+        return lax.rem(me + jnp.where(me < XR, i, 2 * XR - i), count)
+
     def ship(src_ref, dst_ref, sends, recvs, c, at, length):
         span = pl.ds(at, length)
 
         def copy(i):
-            t = lax.rem(me + i, count)
+            t = target(i, c)
             return pltpu.make_async_remote_copy(
                 src_ref=src_ref.at[t, :, span, :],
                 dst_ref=dst_ref.at[me, :, span, :],
                 send_sem=sends.at[c, i],
-                recv_sem=recvs.at[c, i],
+                recv_sem=recvs.at[c, me],
                 device_id=device(t),
                 device_id_type=pl.DeviceIdType.MESH,
             )
 
         def local():
             return pltpu.make_async_copy(
-                src_ref.at[me, :, span, :], dst_ref.at[me, :, span, :], recvs.at[c, 0]
+                src_ref.at[me, :, span, :], dst_ref.at[me, :, span, :], recvs.at[c, me]
             )
 
         return copy, local
@@ -639,26 +642,33 @@
         g = t // 2
         return jnp.logical_and(g != 5, g != XR - 6)
 
+    def goes(t, *args):
+        return jnp.logical_and(t != me, takes(t, *args))
+
     def ship_start(*args):
         copy, local = ship(*args)
 
         def start(i, carry):
-            @pl.when(takes(lax.rem(me + i, count), *args))
+            @pl.when(goes(target(i, args[4]), *args))
             def _():
                 copy(i).start()
             return carry
 
-        lax.fori_loop(1, count, start, 0)
+        lax.fori_loop(0, count, start, 0)
 
         @pl.when(takes(me, *args))
         def _():
             local().start()
 
-    def ship_arrive(*args):
-        copy, local = ship(*args)
+    def ship_arrive(src_ref, dst_ref, sends, recvs, c, at, length):
+        span = pl.ds(at, length)
+        _, local = ship(src_ref, dst_ref, sends, recvs, c, at, length)
 
         def wait(i, carry):
-            copy(i).wait_recv()
+            t = lax.rem(me + i, count)
+            pltpu.make_async_copy(
+                src_ref.at[t, :, span, :], dst_ref.at[t, :, span, :], recvs.at[c, t]
+            ).wait()
             return carry
 
         lax.fori_loop(1, count, wait, 0)
@@ -668,12 +678,12 @@
         copy, _ = ship(*args)
 
         def wait(i, carry):
-            @pl.when(takes(lax.rem(me + i, count), *args))
+            @pl.when(goes(target(i, args[4]), *args))
             def _():
                 copy(i).wait_send()
             return carry
 
-        lax.fori_loop(1, count, wait, 0)
+        lax.fori_loop(0, count, wait, 0)
 
     def spread_args(c):
         return out_ref, in_ref, out_send, out_recv, c, offsets[c], CHUNKS[c]

time: 246 us -> 240 us (0.976)
  Pallas kernels: 245 us -> 237 us
    pallas_call x1, Pallas kernels: 241 us -> 234 us  [lines_local(): pl.pallas_call(substep_kernel, out_shape=jax.ShapeDtypeStruct((4, mode_co...]
where the time goes in v4:
time: 240 us; the launch traced here: 239 us
  Pallas kernels  237 us (99%)
    pallas_call x1, Pallas kernels, lines_local(): pl.pallas_call(substep_kernel, out_shape=jax.ShapeDtypeStruct((4, mode_co...  234 us

profile of v4, /device:TPU:12, one launch (start us, length us, event | category | flops | bytes accessed | tf_op | source)
XLA Modules:
  0.0 238.9 jit_solution(10833366168205484431)
XLA Ops:
  1.3 0.0 copy-start
  1.3 0.0 copy-start.1
  1.3 233.7 %substep.1.term_ref = f32[4,256,768]{2,1,0:T(8,128)S(1)} custom-call(f32[4,256,1024]{2,1,0:T(8,128)} %bitcast.9, bf16[48,256,512]{2,1,0:T(8,128)(2,1)} %constant.6.clone.tables_hbm, bf16[16,512,256]{2,1,0:T(8,128)(2,1)} %constant.7.clone.fh_hbm, bf16[16,512,256]{2,1,0:T(8,128)(2,1)} %constant.8.clone.fl_hbm), custom_call_target="tpu_custom_call" | custom-call | flops 10000000000 | bytes 67108864 | tf_op jit(solution)/shard_map/substep/pallas_call | solution.py:885
  235.0 0.0 copy-done
  235.0 0.0 copy-done.1
  235.0 3.7 %advance.1 = (f32[2,2,256,1024]{3,2,1,0:T(8,128)}, f32[2,2,256,1024]{3,2,1,0:T(8,128)}) custom-call(f32[1]{0:T(128)S(6)} %copy.10.base_ref, f32[2,2,256,1024]{3,2,1,0:T(8,128)S(1)} %bitcast.10, f32[2,2,256,1024]{3,2,1,0:T(8,128)S(1)} %bitcast.11, f32[4,256,768]{2,1,0:T(8,128)S(1)} %substep.1.term_ref), custom_call_target="tpu_custom_call" | custom-call | tf_op jit(solution)/shard_map/advance/pallas_call | solution.py:930
Async XLA Ops:
  1.3 233.7 %copy-start = (f32[2,2,1,256,1024]{4,3,2,1,0:T(8,128)S(1)}, f32[2,2,1,256,1024]{4,3,2,1,0:T(8,128)}, u32[]{:S(2)}) copy-start(f32[2,2,1,256,1024]{4,3,2,1,0:T(8,128)} %param.6) | copy-start | bytes 12582916
  1.3 233.7 %copy-start.1 = (f32[2,2,1,256,1024]{4,3,2,1,0:T(8,128)S(1)}, f32[2,2,1,256,1024]{4,3,2,1,0:T(8,128)}, u32[]{:S(2)}) copy-start(f32[2,2,1,256,1024]{4,3,2,1,0:T(8,128)} %param.7) | copy-start | bytes 12582916

commit v5 on v4

--- a/solution.py
+++ b/solution.py
@@ -208,7 +208,7 @@
 LOW = (0, 1, 2)
 HIGH = (5, 6, 7)
 MIB = 1 << 20
-CHUNKS = (16,) * 8
+CHUNKS = (16, 16, 32, 32, 32)
 UNIT = 8
 UNITS = 11
 SIDE = 16 * UNITS
@@ -222,7 +222,7 @@
 UNROLL_FWD = 8
 UNROLL_EARLY = 4
 BLOCK = 32
-SUB_VMEM = 49
+SUB_VMEM = 49.5
 ADV_VMEM = 40
 SHORT = 9
 NEEDED = SIDE - 4

time: 240 us -> 239 us (level)
  no operation moved by 1% of the time
where the time goes in v5:
time: 239 us; the launch traced here: 237 us
  Pallas kernels  236 us (99%)
    pallas_call x1, Pallas kernels, lines_local(): pl.pallas_call(substep_kernel, out_shape=jax.ShapeDtypeStruct((4, mode_co...  232 us

profile of v5, /device:TPU:12, one launch (start us, length us, event | category | flops | bytes accessed | tf_op | source)
XLA Modules:
  0.0 237.4 jit_solution(17376937238843205844)
XLA Ops:
  1.3 0.0 copy-start
  1.3 0.0 copy-start.1
  1.3 232.3 %substep.1.term_ref = f32[4,256,768]{2,1,0:T(8,128)S(1)} custom-call(f32[4,256,1024]{2,1,0:T(8,128)} %bitcast.9, bf16[48,256,512]{2,1,0:T(8,128)(2,1)} %constant.6.clone.tables_hbm, bf16[16,512,256]{2,1,0:T(8,128)(2,1)} %constant.7.clone.fh_hbm, bf16[16,512,256]{2,1,0:T(8,128)(2,1)} %constant.8.clone.fl_hbm), custom_call_target="tpu_custom_call" | custom-call | flops 10000000000 | bytes 67108864 | tf_op jit(solution)/shard_map/substep/pallas_call | solution.py:885
  233.6 0.0 copy-done
  233.6 0.0 copy-done.1
  233.6 3.7 %advance.1 = (f32[2,2,256,1024]{3,2,1,0:T(8,128)}, f32[2,2,256,1024]{3,2,1,0:T(8,128)}) custom-call(f32[1]{0:T(128)S(6)} %copy.10.base_ref, f32[2,2,256,1024]{3,2,1,0:T(8,128)S(1)} %bitcast.10, f32[2,2,256,1024]{3,2,1,0:T(8,128)S(1)} %bitcast.11, f32[4,256,768]{2,1,0:T(8,128)S(1)} %substep.1.term_ref), custom_call_target="tpu_custom_call" | custom-call | tf_op jit(solution)/shard_map/advance/pallas_call | solution.py:930
Async XLA Ops:
  1.3 232.3 %copy-start = (f32[2,2,1,256,1024]{4,3,2,1,0:T(8,128)S(1)}, f32[2,2,1,256,1024]{4,3,2,1,0:T(8,128)}, u32[]{:S(2)}) copy-start(f32[2,2,1,256,1024]{4,3,2,1,0:T(8,128)} %param.6) | copy-start | bytes 12582916
  1.3 232.3 %copy-start.1 = (f32[2,2,1,256,1024]{4,3,2,1,0:T(8,128)S(1)}, f32[2,2,1,256,1024]{4,3,2,1,0:T(8,128)}, u32[]{:S(2)}) copy-start(f32[2,2,1,256,1024]{4,3,2,1,0:T(8,128)} %param.7) | copy-start | bytes 12582916

commit v6 on v5

--- a/solution.py
+++ b/solution.py
@@ -216,7 +216,7 @@
 OWN = 2 * UNITS
 EXTRA = PER - OWN
 SPANS = (3, 3, 3, 1, 1)
-BACK_AHEAD = 3
+BACK_AHEAD = 4
 UNROLL = 16
 UNROLL_INV = 8
 UNROLL_FWD = 8

time: 239 us -> 239 us (level)
  no operation moved by 1% of the time
where the time goes in v6:
time: 239 us; the launch traced here: 237 us
  Pallas kernels  236 us (99%)
    pallas_call x1, Pallas kernels, lines_local(): pl.pallas_call(substep_kernel, out_shape=jax.ShapeDtypeStruct((4, mode_co...  232 us

profile of v6, /device:TPU:12, one launch (start us, length us, event | category | flops | bytes accessed | tf_op | source)
XLA Modules:
  0.0 237.1 jit_solution(14081372653664582348)
XLA Ops:
  1.3 0.0 copy-start
  1.3 0.0 copy-start.1
  1.3 232.0 %substep.1.term_ref = f32[4,256,768]{2,1,0:T(8,128)S(1)} custom-call(f32[4,256,1024]{2,1,0:T(8,128)} %bitcast.9, bf16[48,256,512]{2,1,0:T(8,128)(2,1)} %constant.6.clone.tables_hbm, bf16[16,512,256]{2,1,0:T(8,128)(2,1)} %constant.7.clone.fh_hbm, bf16[16,512,256]{2,1,0:T(8,128)(2,1)} %constant.8.clone.fl_hbm), custom_call_target="tpu_custom_call" | custom-call | flops 10000000000 | bytes 67108864 | tf_op jit(solution)/shard_map/substep/pallas_call | solution.py:885
  233.3 0.0 copy-done
  233.3 0.0 copy-done.1
  233.3 3.7 %advance.1 = (f32[2,2,256,1024]{3,2,1,0:T(8,128)}, f32[2,2,256,1024]{3,2,1,0:T(8,128)}) custom-call(f32[1]{0:T(128)S(6)} %copy.10.base_ref, f32[2,2,256,1024]{3,2,1,0:T(8,128)S(1)} %bitcast.10, f32[2,2,256,1024]{3,2,1,0:T(8,128)S(1)} %bitcast.11, f32[4,256,768]{2,1,0:T(8,128)S(1)} %substep.1.term_ref), custom_call_target="tpu_custom_call" | custom-call | tf_op jit(solution)/shard_map/advance/pallas_call | solution.py:930
Async XLA Ops:
  1.3 232.0 %copy-start = (f32[2,2,1,256,1024]{4,3,2,1,0:T(8,128)S(1)}, f32[2,2,1,256,1024]{4,3,2,1,0:T(8,128)}, u32[]{:S(2)}) copy-start(f32[2,2,1,256,1024]{4,3,2,1,0:T(8,128)} %param.6) | copy-start | bytes 12582916
  1.3 232.0 %copy-start.1 = (f32[2,2,1,256,1024]{4,3,2,1,0:T(8,128)S(1)}, f32[2,2,1,256,1024]{4,3,2,1,0:T(8,128)}, u32[]{:S(2)}) copy-start(f32[2,2,1,256,1024]{4,3,2,1,0:T(8,128)} %param.7) | copy-start | bytes 12582916
